TPU v7x, 256 devices: a whole 4x4x8 slice. The times are simulated.
256 devices in a mesh: dp: 16 (over z, y_hi), fsdp: 16 (over y_lo, x, core).
Axes of the slice: x: 4, y: 4 (y_hi: 2, y_lo: 2; y = y_hi * 2 + y_lo), z: 8, core: 2. Of those that a mesh axis runs over, the one named last changes fastest.
Arguments:
- hidden_input: bfloat16 [2048, 32, 8192], P(('dp', 'fsdp')), may hold values from -6 to 6
- input_norm_gain: float32 [8192], replicated, may hold values from 0.8 to 3
- joined_weight: bfloat16 [8192, 768], P('fsdp'), may hold values from -0.0625 to 0.0625
- joined_bias: bfloat16 [768], replicated, may hold values from -3 to 3
- adapter_down: bfloat16 [8192, 64], replicated, may hold values from -0.0625 to 0.0625
- adapter_up: bfloat16 [64, 512], replicated, may hold values from -0.75 to 0.75
- advantage: float32 [2048], P(('dp', 'fsdp')), may hold values from -4 to 4
- output_gradient: bfloat16 [2048, 32, 512], P(('dp', 'fsdp')), may hold values from -6 to 6
- lengths: int32 [2048], P(('dp', 'fsdp')), may hold values from 1 to 32, as said below
- assignment: int32 [2048], P(('dp', 'fsdp')), may hold values from 0 to 15, as said below
Outputs:
- att_out: bfloat16 [2048, 32, 512], P(('dp', 'fsdp'))
- down_gradient: float32 [8192, 64], P('dp')
- up_gradient: float32 [64, 512], P(None, 'dp')
Inputs may be any that keep to these rules, and one draw needn't show every extreme that they name: `assignment`: among the rollouts of the devices that share one fsdp index, every dp index is named by exactly 8 of them, and the 8 rollouts of one device name different dp indices. `lengths`: every device holds a rollout of length 32.
All inputs are finite; a program needn't handle non-finite values.
Results may differ from a plain program's by a relative error of at most 0.02.
The roundings to bfloat16 on the way count: a program that leaves them out, or rounds other values in their place, can miss the bound.
Values may be sent and summed in bfloat16 or wider, within the bound.
A program may use at most 128 MiB of HBM per device.

v0:
```python
import jax
import jax.numpy as jnp
from jax import lax
from jax.sharding import PartitionSpec as P

EPSILON = 1e-06
ADAPTER_SCALE = 2.0


def normalize(hidden_rows, gain):
    hidden_wide = hidden_rows.astype(jnp.float32)
    scale_rows = lax.rsqrt(jnp.mean(hidden_wide * hidden_wide, axis=-1, keepdims=True) + EPSILON)
    return (hidden_wide * scale_rows * gain).astype(jnp.bfloat16)


def weigh_grad(gradient_rows, adv_rows, length_rows):
    factor = adv_rows / length_rows.astype(jnp.float32)
    return (gradient_rows.astype(jnp.float32) * factor[:, None, None]).astype(jnp.bfloat16)


def attention(query_rows, keys_rows, values_rows, input_lengths):
    rollouts_here = input_lengths.shape[0]
    slot_len = query_rows.shape[0] // rollouts_here
    head_size = keys_rows.shape[1]
    num_heads = query_rows.shape[1] // head_size
    query_four = query_rows.reshape(rollouts_here, slot_len, num_heads, head_size).astype(
        jnp.float32
    )
    key_three = keys_rows.reshape(rollouts_here, slot_len, head_size).astype(jnp.float32)
    value_three = values_rows.reshape(rollouts_here, slot_len, head_size).astype(jnp.float32)
    scores = jnp.einsum("rqhd,rkd->rhqk", query_four, key_three) * head_size ** (-0.5)
    position = jnp.arange(slot_len, dtype=jnp.int32)
    visible = (position[None, None, None, :] <= position[None, None, :, None]) & (
        position[None, None, None, :] < input_lengths[:, None, None, None]
    )
    scores = jnp.where(visible, scores, jnp.float32(-1e30))
    row_max = jnp.max(scores, axis=-1, keepdims=True)
    raised = jnp.exp(scores - row_max)
    weights_soft = (raised / jnp.sum(raised, axis=-1, keepdims=True)).astype(jnp.bfloat16)
    attention_output = jnp.einsum("rhqk,rkd->rqhd", weights_soft.astype(jnp.float32), value_three)
    live_rows = (position[None, :] < input_lengths[:, None])[:, :, None, None]
    attention_output = jnp.where(live_rows, attention_output, jnp.float32(0.0))
    return attention_output.astype(jnp.bfloat16).reshape(
        rollouts_here * slot_len, num_heads * head_size
    )


def learner_block_step(
    normalized_rows, projected_rows, gradient_rows, input_lengths, adapter_down, adapter_up
):
    query_total_width = adapter_up.shape[1]
    head_size = (projected_rows.shape[1] - query_total_width) // 2
    adapter_lowrank = jnp.dot(
        normalized_rows, adapter_down, preferred_element_type=jnp.float32
    ).astype(jnp.bfloat16)
    query_rows = (
        projected_rows[:, :query_total_width]
        + ADAPTER_SCALE * jnp.dot(adapter_lowrank, adapter_up, preferred_element_type=jnp.float32)
    ).astype(jnp.bfloat16)
    keys_rows = projected_rows[:, query_total_width : query_total_width + head_size].astype(
        jnp.bfloat16
    )
    values_rows = projected_rows[:, query_total_width + head_size :].astype(jnp.bfloat16)
    attention_output, pullback = jax.vjp(
        lambda query_in: attention(query_in, keys_rows, values_rows, input_lengths), query_rows
    )
    query_gradient = pullback(gradient_rows)[0]
    up_gradient = ADAPTER_SCALE * lax.dot_general(
        adapter_lowrank,
        query_gradient,
        (((0,), (0,)), ((), ())),
        preferred_element_type=jnp.float32,
    )
    lowrank_gradient = (
        ADAPTER_SCALE
        * lax.dot_general(
            query_gradient, adapter_up, (((1,), (1,)), ((), ())), preferred_element_type=jnp.float32
        )
    ).astype(jnp.bfloat16)
    down_gradient = lax.dot_general(
        normalized_rows,
        lowrank_gradient,
        (((0,), (0,)), ((), ())),
        preferred_element_type=jnp.float32,
    )
    return (attention_output, down_gradient, up_gradient)


def on_device(
    hidden_input,
    input_norm_gain,
    joined_weight,
    joined_bias,
    adapter_down,
    adapter_up,
    advantage,
    output_gradient,
    lengths,
    assignment,
):
    rollouts_here, slot_len, model_width = hidden_input.shape
    dp_size = lax.axis_size("dp")
    query_total_width = adapter_up.shape[1]
    weighted_grad = weigh_grad(output_gradient, advantage, lengths)
    targets = assignment[None, :] == jnp.arange(dp_size, dtype=jnp.int32)[:, None]
    slot_lengths = jnp.sum(jnp.where(targets, lengths[None, :], 0), axis=1)

    def to_slots(values):
        select_table = targets.astype(values.dtype)
        flat_rows = values.reshape(rollouts_here, -1)
        moved = jnp.dot(select_table, flat_rows, preferred_element_type=jnp.float32).astype(
            values.dtype
        )
        return moved.reshape((dp_size,) + values.shape[1:])

    arrived_hidden, arrived_grad, arrived_len = (
        lax.all_to_all(to_slots(hidden_input), "dp", split_axis=0, concat_axis=0, tiled=True),
        lax.all_to_all(to_slots(weighted_grad), "dp", split_axis=0, concat_axis=0, tiled=True),
        lax.all_to_all(slot_lengths, "dp", split_axis=0, concat_axis=0, tiled=True),
    )
    arrays = (arrived_hidden, arrived_grad)
    filled = arrived_len > 0
    slot_rank = jnp.cumsum(filled.astype(jnp.int32)) - 1
    select_table = (
        slot_rank[None, :] == jnp.arange(rollouts_here, dtype=jnp.int32)[:, None]
    ) & filled[None, :]
    picked = tuple(
        (
            jnp.dot(
                select_table.astype(values.dtype),
                values.reshape(dp_size, -1),
                preferred_element_type=jnp.float32,
            )
            .astype(values.dtype)
            .reshape((rollouts_here,) + values.shape[1:])
            for values in arrays
        )
    )
    kept_lengths = jnp.sum(jnp.where(select_table, arrived_len[None, :], 0), axis=1).astype(
        jnp.int32
    )
    (local_hidden, local_grad), local_len = (picked, kept_lengths)
    normalized_rows = normalize(local_hidden, input_norm_gain).reshape(-1, model_width)
    projected_rows = jnp.dot(
        normalized_rows,
        lax.all_gather(joined_weight, "fsdp", axis=0, tiled=True),
        preferred_element_type=jnp.float32,
    ) + joined_bias.astype(jnp.float32)
    attention_output, down_gradient, up_gradient = learner_block_step(
        normalized_rows,
        projected_rows,
        local_grad.reshape(normalized_rows.shape[0], query_total_width),
        local_len,
        adapter_down,
        adapter_up,
    )
    att_out = attention_output.reshape(rollouts_here, slot_len, query_total_width)
    column_a, column_b = lax.psum((down_gradient, up_gradient), "fsdp")
    share_a, share_b = (
        lax.psum_scatter(column_a, "dp", scatter_dimension=0, tiled=True),
        lax.psum_scatter(column_b, "dp", scatter_dimension=1, tiled=True),
    )
    return (att_out, share_a, share_b)


def solution(mesh):
    in_specs = (
        P(("dp", "fsdp"), None, None),
        P(),
        P("fsdp", None),
        P(),
        P(),
        P(),
        P(("dp", "fsdp")),
        P(("dp", "fsdp"), None, None),
        P(("dp", "fsdp")),
        P(("dp", "fsdp")),
    )
    out_specs = (P(("dp", "fsdp"), None, None), P("dp", None), P(None, "dp"))
    return jax.shard_map(
        on_device, mesh=mesh, in_specs=in_specs, out_specs=out_specs, check_vma=False
    )
```

profile of v0, /device:TPU:1, one launch (start us, length us, event | category | flops | bytes accessed | tf_op | source)
XLA Modules:
  0.0 849.1 jit_solution(1667598884189132958)
XLA Ops:
  7.2 0.7 all-gather.2.cloned.1.call-update
  7.9 0.8 select_reduce_fusion.1
  8.7 0.7 copy.51
  9.4 11.7 %all-to-all-start = ((s32[16,1,1]{2,1,0:T(1,128)}), s32[16,1,1]{2,1,0:T(1,128)S(1)}, u32[]{:S(2)}, u32[]{:S(2)}) async-start(s32[16,1,1]{2,1,0:T(1,128)} %copy.51), calls=%async_computation | async-start | bytes 16384 | tf_op jit(solution)/shard_map/all_to_all | solution.py:119
  21.1 0.7 convert_divide_fusion
  21.8 1.1 fusion.18
  23.0 1.1 convolution_convert_fusion.2
  24.1 1.0 copy.69
  25.1 4.8 all-to-all-done
  29.9 4.2 all-to-all-start.2
  34.2 4.6 copy.65
  38.8 5.3 convolution_convert_fusion
  44.1 11.3 %copy.66 = bf16[2,8,32,8192]{3,2,1,0:T(8,128)(2,1)} copy(bf16[2,8,32,8192]{3,1,2,0:T(8,128)(2,1)} %bitcast.100) | data formatting | bytes 16777216
  55.4 9.1 %all-to-all-start.1 = ((bf16[16,32,8192]{2,1,0:T(8,128)(2,1)}), bf16[16,32,8192]{2,1,0:T(8,128)(2,1)}, u32[]{:S(2)}, u32[]{:S(2)}) async-start(bf16[16,32,8192]{2,1,0:T(8,128)(2,1)} %bitcast.103), calls=%async_computation.1 | async-start | bytes 16777216 | tf_op jit(solution)/shard_map/all_to_all | solution.py:117
  66.2 190.3 %all-to-all-done.1 = bf16[16,32,8192]{2,1,0:T(8,128)(2,1)} async-done(((bf16[16,32,8192]{2,1,0:T(8,128)(2,1)}), bf16[16,32,8192]{2,1,0:T(8,128)(2,1)}, u32[]{:S(2)}, u32[]{:S(2)}) %all-to-all-start.1) | async-done | bytes 8388640 | tf_op jit(solution)/shard_map/all_to_all | solution.py:117
  256.6 11.2 %copy.67 = bf16[2,8,32,8192]{3,1,2,0:T(8,128)(2,1)} copy(bf16[2,8,32,8192]{3,2,1,0:T(8,128)(2,1)} %bitcast.29) | data formatting | bytes 16777216
  267.8 10.6 %fusion.55 = (f32[8,262144]{1,0:T(8,128)}, f32[8,262144]{1,0:T(8,128)}) fusion(bf16[16,262144]{1,0:T(8,128)(2,1)} %bitcast.102, s32[16]{0:T(128)S(1)} %add_reduce_fusion, pred[16]{0:T(512)(128)(4,1)S(1)} %broadcast_compare_fusion), kind=kOutput, calls=%fused_computation.91 | convolution fusion | flops 73400576 | bytes 25165904 | tf_op jit(solution)/shard_map/dot_general | solution.py:129
  278.4 8.1 reshape.209
  286.5 3.9 reduce_sum.73
  290.5 4.5 multiply_convert_fusion
  295.0 1.9 copy-done.1
  297.0 1.4 convolution_convert_fusion.6
  298.4 9.1 %fusion.56 = (bf16[256,768]{1,0:T(8,128)(2,1)S(1)}, f32[256,768]{1,0:T(8,128)S(1)}) fusion(f32[768]{0:T(1024)S(1)} %convert_element_type.115, bf16[256,8192]{1,0:T(8,128)(2,1)} %copy-done.1, bf16[8192,768]{1,0:T(8,128)(2,1)} %all-gather.2.cloned.1.call-done), kind=kOutput, calls=%fused_computation.92 | convolution fusion | flops 3221618688 | bytes 17959936 | tf_op jit(solution)/shard_map/dot_general | solution.py:144
  308.6 0.6 multiply_reduce_fusion.1
  310.2 4.7 fusion.7
  314.9 1.0 convolution_multiply_fusion.2
  316.0 197.9 %reduce-scatter.3.cloned.1.call-done = f32[512,64]{0,1:T(8,128)} async-done(((f32[8192,64]{0,1:T(8,128)}), f32[512,64]{0,1:T(8,128)}) %reduce-scatter.3.cloned.1.call-update) | async-done | bytes 131088 | tf_op jit(solution)/shard_map/reduce_scatter | solution.py:160
  514.3 0.7 copy.92
  515.1 199.7 %reduce-scatter.5.cloned.1.call-done = f32[64,32]{0,1:T(8,128)} async-done(((f32[64,512]{0,1:T(8,128)}), f32[64,32]{0,1:T(8,128)}) %reduce-scatter.5.cloned.1.call-update) | async-done | bytes 8208 | tf_op jit(solution)/shard_map/reduce_scatter | solution.py:161
  714.8 54.3 %psum.17 = f32[64,32]{0,1:T(8,128)} all-reduce(f32[64,32]{0,1:T(8,128)} %reduce-scatter.5.cloned.1.call-done), channel_id=1, replica_groups=mesh['dp'=16,'fsdp'=16] {'fsdp'}, use_global_device_ids=true, to_apply=%region_11.12 | all-reduce | flops 2048 | bytes 16384 | tf_op jit(solution)/shard_map/psum | solution.py:158
  769.1 72.0 %all-reduce.2.cloned.1.call-done = f32[512,64]{0,1:T(8,128)} async-done(((f32[512,64]{0,1:T(8,128)}), f32[512,64]{0,1:T(8,128)}) %all-reduce.2.cloned.1.call-update) | async-done | bytes 131088 | tf_op jit(solution)/shard_map/psum | solution.py:158
  841.0 1.6 copy.94
  (50 shorter events, 4.6 us)
Async XLA Ops:
  7.2 289.8 %copy-start = (bf16[8192,64]{0,1:T(8,128)(2,1)S(1)}, bf16[8192,64]{0,1:T(8,128)(2,1)}, u32[]{:S(2)}) copy-start(bf16[8192,64]{0,1:T(8,128)(2,1)} %param.14) | copy-start | bytes 3145732
  7.2 31.6 %copy-start.5 = (s32[8]{0:T(128)S(1)}, s32[8]{0:T(128)}, u32[]{:S(2)}) copy-start(s32[8]{0:T(128)} %param.19) | copy-start | bytes 100
  7.2 291.2 %all-gather.2.cloned.1.call-start = ((), (), s32[]{:S(2)}) async-start(), calls=%async_computation.5 | async-start | bytes 13369344 | tf_op jit(solution)/shard_map/all_gather | solution.py:146
  9.4 20.5 %all-to-all-start = ((s32[16,1,1]{2,1,0:T(1,128)}), s32[16,1,1]{2,1,0:T(1,128)S(1)}, u32[]{:S(2)}, u32[]{:S(2)}) async-start(s32[16,1,1]{2,1,0:T(1,128)} %copy.51), calls=%async_computation | async-start | bytes 16384 | tf_op jit(solution)/shard_map/all_to_all | solution.py:119
  29.9 25.5 %all-to-all-start.2 = ((bf16[16,32,512]{2,1,0:T(8,128)(2,1)}), bf16[16,32,512]{2,1,0:T(8,128)(2,1)S(1)}, u32[]{:S(2)}, u32[]{:S(2)}) async-start(bf16[16,32,512]{2,1,0:T(8,128)(2,1)} %bitcast.34), calls=%async_computation.2 | async-start | bytes 1048576 | tf_op jit(solution)/shard_map/all_to_all | solution.py:118
  55.4 9.3 %copy-start.4 = (bf16[768]{0:T(1024)(128)(2,1)S(1)}, bf16[768]{0:T(1024)(128)(2,1)}, u32[]{:S(2)}) copy-start(bf16[768]{0:T(1024)(128)(2,1)} %param.13) | copy-start | bytes 4612
  55.4 201.2 %all-to-all-start.1 = ((bf16[16,32,8192]{2,1,0:T(8,128)(2,1)}), bf16[16,32,8192]{2,1,0:T(8,128)(2,1)}, u32[]{:S(2)}, u32[]{:S(2)}) async-start(bf16[16,32,8192]{2,1,0:T(8,128)(2,1)} %bitcast.103), calls=%async_computation.1 | async-start | bytes 16777216 | tf_op jit(solution)/shard_map/all_to_all | solution.py:117
  64.5 449.5 %reduce-scatter.3.cloned.1.call-start = ((), (), s32[]{:S(2)}) async-start(), calls=%async_computation.6 | async-start | bytes 2228224 | tf_op jit(solution)/shard_map/reduce_scatter | solution.py:160
  286.5 4.0 copy-start.3
  295.0 2.0 copy-start.1
  298.4 9.1 %copy-start.2 = (bf16[64,512]{1,0:T(8,128)(2,1)S(1)}, bf16[64,512]{1,0:T(8,128)(2,1)}, u32[]{:S(2)}) copy-start(bf16[64,512]{1,0:T(8,128)(2,1)} %param.15) | copy-start | bytes 196612
  314.9 399.9 %reduce-scatter.5.cloned.1.call-start = ((), (), s32[]{:S(2)}) async-start(), calls=%async_computation.8 | async-start | bytes 278528 | tf_op jit(solution)/shard_map/reduce_scatter | solution.py:161
  316.0 525.1 %all-reduce.2.cloned.1.call-start = ((), (), s32[]{:S(2)}) async-start(), calls=%async_computation.7 | async-start | bytes 262144 | tf_op jit(solution)/shard_map/psum | solution.py:158
Sparse Core Ops, SparseCore 0:
  9.9 95.4 all-gather.1
  315.0 198.9 reduce-scatter.2
  517.8 196.9 reduce-scatter.4
  717.4 123.5 all-reduce.1
where the time goes:
time: 850 us; the launch traced here: 849 us
  waiting for transfers between devices  666 us (78%)
  blocking collectives  54.3 us (6%)
  local copies, waits for them, and re-layouts  41.9 us (5%)
  matrix products  35.5 us (4%)
  starting transfers between devices  25.4 us (3%)
  between operations  14 us (2%)
  other arithmetic  12.4 us (1%)
    reduce_scatter x1, waiting for transfers between devices, on_device(): lax.psum_scatter(column_b, 'dp', scatter_dimension=1, tiled=True)  200 us
    reduce_scatter x1, waiting for transfers between devices, on_device(): lax.psum_scatter(column_a, 'dp', scatter_dimension=0, tiled=True)  198 us
    all_to_all x1, waiting for transfers between devices, on_device(): lax.all_to_all(to_slots(hidden_input), 'dp', split_axis=0, concat_axis=0,...  190 us
    psum x1, waiting for transfers between devices, on_device(): column_a, column_b = lax.psum((down_gradient, up_gradient), 'fsdp')  72 us
    psum x1, blocking collectives, on_device(): column_a, column_b = lax.psum((down_gradient, up_gradient), 'fsdp')  54.3 us
    unnamed x19, local copies, waits for them, and re-layouts  32.1 us
  transfers between devices with their start and end apart: 7, of which 5 were waited for; matrix products, arithmetic and copies ran while one was open for 8% of the time, Pallas kernels for 0%

commit v1 on v0

--- a/solution.py
+++ b/solution.py
@@ -102,45 +102,7 @@
     dp_size = lax.axis_size("dp")
     query_total_width = adapter_up.shape[1]
     weighted_grad = weigh_grad(output_gradient, advantage, lengths)
-    targets = assignment[None, :] == jnp.arange(dp_size, dtype=jnp.int32)[:, None]
-    slot_lengths = jnp.sum(jnp.where(targets, lengths[None, :], 0), axis=1)
-
-    def to_slots(values):
-        select_table = targets.astype(values.dtype)
-        flat_rows = values.reshape(rollouts_here, -1)
-        moved = jnp.dot(select_table, flat_rows, preferred_element_type=jnp.float32).astype(
-            values.dtype
-        )
-        return moved.reshape((dp_size,) + values.shape[1:])
-
-    arrived_hidden, arrived_grad, arrived_len = (
-        lax.all_to_all(to_slots(hidden_input), "dp", split_axis=0, concat_axis=0, tiled=True),
-        lax.all_to_all(to_slots(weighted_grad), "dp", split_axis=0, concat_axis=0, tiled=True),
-        lax.all_to_all(slot_lengths, "dp", split_axis=0, concat_axis=0, tiled=True),
-    )
-    arrays = (arrived_hidden, arrived_grad)
-    filled = arrived_len > 0
-    slot_rank = jnp.cumsum(filled.astype(jnp.int32)) - 1
-    select_table = (
-        slot_rank[None, :] == jnp.arange(rollouts_here, dtype=jnp.int32)[:, None]
-    ) & filled[None, :]
-    picked = tuple(
-        (
-            jnp.dot(
-                select_table.astype(values.dtype),
-                values.reshape(dp_size, -1),
-                preferred_element_type=jnp.float32,
-            )
-            .astype(values.dtype)
-            .reshape((rollouts_here,) + values.shape[1:])
-            for values in arrays
-        )
-    )
-    kept_lengths = jnp.sum(jnp.where(select_table, arrived_len[None, :], 0), axis=1).astype(
-        jnp.int32
-    )
-    (local_hidden, local_grad), local_len = (picked, kept_lengths)
-    normalized_rows = normalize(local_hidden, input_norm_gain).reshape(-1, model_width)
+    normalized_rows = normalize(hidden_input, input_norm_gain).reshape(-1, model_width)
     projected_rows = jnp.dot(
         normalized_rows,
         lax.all_gather(joined_weight, "fsdp", axis=0, tiled=True),
@@ -149,12 +111,29 @@
     attention_output, down_gradient, up_gradient = learner_block_step(
         normalized_rows,
         projected_rows,
-        local_grad.reshape(normalized_rows.shape[0], query_total_width),
-        local_len,
+        weighted_grad.reshape(normalized_rows.shape[0], query_total_width),
+        lengths,
         adapter_down,
         adapter_up,
     )
-    att_out = attention_output.reshape(rollouts_here, slot_len, query_total_width)
+    targets = assignment[None, :] == jnp.arange(dp_size, dtype=jnp.int32)[:, None]
+    slots = jnp.dot(
+        targets.astype(jnp.bfloat16),
+        attention_output.reshape(rollouts_here, -1),
+        preferred_element_type=jnp.float32,
+    ).astype(jnp.bfloat16)
+    arrived = lax.all_to_all(slots, "dp", split_axis=0, concat_axis=0, tiled=True)
+    sent = jnp.sum(targets.astype(jnp.int32), axis=1)
+    filled = lax.all_to_all(sent, "dp", split_axis=0, concat_axis=0, tiled=True) > 0
+    slot_rank = jnp.cumsum(filled.astype(jnp.int32)) - 1
+    select_table = (
+        slot_rank[None, :] == jnp.arange(rollouts_here, dtype=jnp.int32)[:, None]
+    ) & filled[None, :]
+    att_out = (
+        jnp.dot(select_table.astype(jnp.bfloat16), arrived, preferred_element_type=jnp.float32)
+        .astype(jnp.bfloat16)
+        .reshape(rollouts_here, slot_len, query_total_width)
+    )
     column_a, column_b = lax.psum((down_gradient, up_gradient), "fsdp")
     share_a, share_b = (
         lax.psum_scatter(column_a, "dp", scatter_dimension=0, tiled=True),

time: 850 us -> 639 us (0.75)
  waiting for transfers between devices: 666 us -> 521 us
  local copies, waits for them, and re-layouts: 41.9 us -> 7.78 us
  matrix products: 35.5 us -> 19.1 us
  starting transfers between devices: 25.4 us -> 13.4 us
    all_to_all x3 -> x2, waiting for transfers between devices: 195 us -> 4.99 us  [the longest x1 4.99 us: on_device(): lax.all_to_all(sent, 'dp', split_axis=0, concat_axis=0, tiled=True) > 0]
    all_gather x1, waiting for transfers between devices: 0.02 us -> 70.2 us  [on_device(): lax.all_gather(joined_weight, 'fsdp', axis=0, tiled=True)]
    psum x1, waiting for transfers between devices: 72 us -> 124 us  [on_device(): column_a, column_b = lax.psum((down_gradient, up_gradient), 'fsdp')]
    reduce_scatter x1, waiting for transfers between devices: 198 us -> 152 us  [on_device(): lax.psum_scatter(column_a, 'dp', scatter_dimension=0, tiled=True)]
    reduce_scatter x1, waiting for transfers between devices: 200 us -> 169 us  [on_device(): lax.psum_scatter(column_b, 'dp', scatter_dimension=1, tiled=True)]
    unnamed x19 -> x18, local copies, waits for them, and re-layouts: 32.1 us -> 6.04 us
    dot_general x4 -> x2, matrix products: 17.2 us -> 1.07 us  [the longest x1 0.66 us: on_device(): jnp.dot(select_table.astype(jnp.bfloat16), arrived, preferred_element_typ...]
    all_to_all x3 -> x2, starting transfers between devices: 25.1 us -> 13.2 us  [the longest x1 9.15 us: on_device(): lax.all_to_all(sent, 'dp', split_axis=0, concat_axis=0, tiled=True) > 0]
  transfers between devices with their start and end apart: 7 -> 6, of which waited for: 5 -> 5; matrix products, arithmetic and copies ran while one was open for 8% -> 3% of each run, Pallas kernels for 0% -> 0%
where the time goes in v1:
time: 639 us
  waiting for transfers between devices  521 us (82%)
  blocking collectives  54.4 us (9%)
  matrix products  19.1 us (3%)
  between operations  14 us (2%)
  starting transfers between devices  13.4 us (2%)
  other arithmetic  9.16 us (1%)
  local copies, waits for them, and re-layouts  7.78 us (1%)
    reduce_scatter x1, waiting for transfers between devices, on_device(): lax.psum_scatter(column_b, 'dp', scatter_dimension=1, tiled=True)  169 us
    reduce_scatter x1, waiting for transfers between devices, on_device(): lax.psum_scatter(column_a, 'dp', scatter_dimension=0, tiled=True)  152 us
    psum x1, waiting for transfers between devices, on_device(): column_a, column_b = lax.psum((down_gradient, up_gradient), 'fsdp')  124 us
    all_gather x1, waiting for transfers between devices, on_device(): lax.all_gather(joined_weight, 'fsdp', axis=0, tiled=True)  70.2 us
    psum x1, blocking collectives, on_device(): column_a, column_b = lax.psum((down_gradient, up_gradient), 'fsdp')  54.4 us
  transfers between devices with their start and end apart: 6, of which 5 were waited for; matrix products, arithmetic and copies ran while one was open for 3% of the time, Pallas kernels for 0%

profile of v1, /device:TPU:1, one launch (start us, length us, event | category | flops | bytes accessed | tf_op | source)
XLA Modules:
  0.0 639.0 jit_solution(3077369118089452657)
XLA Ops:
  7.2 0.7 all-gather.2.cloned.1.call-update
  8.0 0.8 convert_element_type.99
  8.8 0.9 iota_compare_fusion.2
  9.8 0.7 convert_divide_fusion
  10.4 3.1 fusion.1
  13.8 1.2 fusion.3
  15.0 1.9 copy-done.1
  16.9 1.4 convolution_convert_fusion.4
  18.4 70.2 %all-gather.2.cloned.1.call-done = bf16[8192,768]{1,0:T(8,128)(2,1)} async-done(((bf16[512,768]{1,0:T(8,128)(2,1)}), bf16[8192,768]{1,0:T(8,128)(2,1)}) %all-gather.2.cloned.1.call-update) | async-done | bytes 12582928 | tf_op jit(solution)/shard_map/all_gather | solution.py:108
  88.5 8.8 %fusion.57 = (bf16[256,768]{1,0:T(8,128)(2,1)S(1)}, f32[256,768]{1,0:T(8,128)S(1)}) fusion(f32[768]{0:T(1024)S(1)} %convert_element_type.99, bf16[256,8192]{1,0:T(8,128)(2,1)} %bitcast.96, bf16[8192,768]{1,0:T(8,128)(2,1)} %all-gather.2.cloned.1.call-done), kind=kOutput, calls=%fused_computation.91 | convolution fusion | flops 3221618688 | bytes 17959936 | tf_op jit(solution)/shard_map/dot_general | solution.py:106
  97.7 0.5 fusion.24
  98.5 0.6 multiply_reduce_fusion.1
  99.5 0.4 convolution_convert_fusion.2
  100.1 1.0 convolution_multiply_fusion.2
  101.2 4.7 fusion.10
  106.0 0.7 copy.47
  106.6 9.2 %all-to-all-start = ((s32[16,1,1]{2,1,0:T(1,128)}), s32[16,1,1]{2,1,0:T(1,128)S(1)}, u32[]{:S(2)}, u32[]{:S(2)}) async-start(s32[16,1,1]{2,1,0:T(1,128)} %copy.47), calls=%async_computation | async-start | bytes 16384 | tf_op jit(solution)/shard_map/all_to_all | solution.py:127
  116.5 0.4 fusion
  116.9 0.5 broadcast.140
  117.4 1.0 reduce.4
  118.4 1.2 reshape.184
  119.6 5.0 all-to-all-done
  124.6 4.1 all-to-all-start.1
  128.7 0.4 compare_reduce_fusion
  129.2 169.1 %reduce-scatter.5.cloned.1.call-done = f32[64,32]{0,1:T(8,128)} async-done(((f32[64,512]{0,1:T(8,128)}), f32[64,32]{0,1:T(8,128)}) %reduce-scatter.5.cloned.1.call-update) | async-done | bytes 8208 | tf_op jit(solution)/shard_map/reduce_scatter | solution.py:140
  298.3 54.4 %psum.17 = f32[64,32]{0,1:T(8,128)} all-reduce(f32[64,32]{0,1:T(8,128)} %reduce-scatter.5.cloned.1.call-done), channel_id=1, replica_groups=mesh['dp'=16,'fsdp'=16] {'fsdp'}, use_global_device_ids=true, to_apply=%region_10.11 | all-reduce | flops 2048 | bytes 16384 | tf_op jit(solution)/shard_map/psum | solution.py:137
  352.7 0.5 reshape.185
  353.2 152.3 %reduce-scatter.3.cloned.1.call-done = f32[512,64]{0,1:T(8,128)} async-done(((f32[8192,64]{0,1:T(8,128)}), f32[512,64]{0,1:T(8,128)}) %reduce-scatter.3.cloned.1.call-update) | async-done | bytes 131088 | tf_op jit(solution)/shard_map/reduce_scatter | solution.py:139
  505.5 0.7 convolution_convert_fusion.1
  506.2 0.8 copy.56
  507.0 124.0 %all-reduce.2.cloned.1.call-done = f32[512,64]{0,1:T(8,128)} async-done(((f32[512,64]{0,1:T(8,128)}), f32[512,64]{0,1:T(8,128)}) %all-reduce.2.cloned.1.call-update) | async-done | bytes 131088 | tf_op jit(solution)/shard_map/psum | solution.py:137
  630.9 1.6 copy.89
  (41 shorter events, 2.4 us)
Async XLA Ops:
  7.2 9.8 %copy-start = (bf16[8192,64]{0,1:T(8,128)(2,1)S(1)}, bf16[8192,64]{0,1:T(8,128)(2,1)}, u32[]{:S(2)}) copy-start(bf16[8192,64]{0,1:T(8,128)(2,1)} %param.14) | copy-start | bytes 3145732
  7.2 6.6 %copy-start.4 = (f32[8192]{0:T(1024)S(1)}, f32[8192]{0:T(1024)}, u32[]{:S(2)}) copy-start(f32[8192]{0:T(1024)} %param.11) | copy-start | bytes 98308
  7.2 81.3 %all-gather.2.cloned.1.call-start = ((), (), s32[]{:S(2)}) async-start(), calls=%async_computation.4 | async-start | bytes 13369344 | tf_op jit(solution)/shard_map/all_gather | solution.py:108
  7.9 290.4 %reduce-scatter.5.cloned.1.call-start = ((), (), s32[]{:S(2)}) async-start(), calls=%async_computation.7 | async-start | bytes 278528 | tf_op jit(solution)/shard_map/reduce_scatter | solution.py:140
  8.0 5.8 copy-start.2
  15.0 2.0 copy-start.1
  18.3 79.1 %copy-start.3 = (bf16[64,512]{1,0:T(8,128)(2,1)S(1)}, bf16[64,512]{1,0:T(8,128)(2,1)}, u32[]{:S(2)}) copy-start(bf16[64,512]{1,0:T(8,128)(2,1)} %param.15) | copy-start | bytes 196612
  18.4 80.1 %copy-start.6 = (bf16[8,32,512]{2,1,0:T(8,128)(2,1)S(1)}, bf16[8,32,512]{2,1,0:T(8,128)(2,1)}, u32[]{:S(2)}) copy-start(bf16[8,32,512]{2,1,0:T(8,128)(2,1)} %param.17) | copy-start | bytes 786436
  101.1 4.8 copy-start.5
  101.1 404.4 %reduce-scatter.3.cloned.1.call-start = ((), (), s32[]{:S(2)}) async-start(), calls=%async_computation.5 | async-start | bytes 2228224 | tf_op jit(solution)/shard_map/reduce_scatter | solution.py:139
  106.6 17.9 %all-to-all-start = ((s32[16,1,1]{2,1,0:T(1,128)}), s32[16,1,1]{2,1,0:T(1,128)S(1)}, u32[]{:S(2)}, u32[]{:S(2)}) async-start(s32[16,1,1]{2,1,0:T(1,128)} %copy.47), calls=%async_computation | async-start | bytes 16384 | tf_op jit(solution)/shard_map/all_to_all | solution.py:127
  124.6 228.1 %all-to-all-start.1 = ((bf16[16,2,8192]{2,1,0:T(2,128)(2,1)}), bf16[16,2,8192]{2,1,0:T(2,128)(2,1)S(1)}, u32[]{:S(2)}, u32[]{:S(2)}) async-start(bf16[16,2,8192]{2,1,0:T(2,128)(2,1)} %reshape.184), calls=%async_computation.1 | async-start | bytes 1048576 | tf_op jit(solution)/shard_map/all_to_all | solution.py:125
  128.7 502.3 %all-reduce.2.cloned.1.call-start = ((), (), s32[]{:S(2)}) async-start(), calls=%async_computation.6 | async-start | bytes 262144 | tf_op jit(solution)/shard_map/psum | solution.py:137
Sparse Core Ops, SparseCore 0:
  9.9 78.6 all-gather.1
  101.2 197.0 reduce-scatter.4
  302.7 202.7 reduce-scatter.2
  508.1 122.7 all-reduce.1

commit v2 on v1

v2 whole, which is shorter than its diff:
```python
import functools

import jax
import jax.numpy as jnp
from jax import lax
from jax.experimental import pallas as pl
from jax.experimental.pallas import tpu as pltpu
from jax.sharding import PartitionSpec as P

EPSILON = 1e-06
ADAPTER_SCALE = 2.0
MESH = pl.DeviceIdType.MESH
NT = (((1,), (1,)), ((), ()))
TN = (((0,), (0,)), ((), ()))

SCHEDULE = (
    ((0, 1, 0, 2), (1, 3, 0, 6), (2, 0, 1, 0), (3, 0, 1, 4)),
    ((0, 1, 0, 0), (1, 3, 0, 2), (2, 0, 1, 6), (3, 0, 1, 2)),
    ((0, 1, 0, 4), (1, 3, 0, 4), (2, 0, 1, 3), (3, 1, 1, 2), (4, 0, 1, 1), (5, 3, 0, 7)),
    ((0, 1, 0, 6), (1, 3, 0, 0), (2, 1, 1, 0), (3, 0, 1, 5), (4, 0, 1, 7), (5, 1, 0, 3)),
    ((0, 1, 0, 7), (1, 3, 1, 0), (2, 1, 1, 4), (3, 3, 1, 2), (4, 3, 0, 5), (5, 1, 1, 3)),
    ((0, 2, 0, 6), (1, 2, 0, 0), (2, 3, 1, 4), (3, 1, 1, 6), (4, 1, 0, 1), (5, 1, 1, 1)),
    ((0, 1, 0, 5), (1, 2, 0, 2), (2, 3, 1, 7), (3, 3, 1, 6), (4, 3, 1, 1), (5, 1, 1, 5)),
    ((0, 2, 1, 4), (1, 2, 0, 4), (2, 2, 1, 6), (3, 3, 1, 5), (4, 3, 1, 3), (5, 2, 0, 1)),
    ((0, 2, 0, 5), (1, 3, 0, 3), (2, 1, 1, 7), (3, 3, 0, 1), (4, 2, 0, 7), (5, 2, 0, 3)),
    ((0, 2, 1, 3), (1, 2, 1, 2), (2, 2, 1, 1), (3, 2, 1, 0), (4, 2, 1, 7), (5, 2, 1, 5)),
)
ENTRIES = tuple((t,) + e for t, row in enumerate(SCHEDULE) for e in row)
N_ENTRIES = len(ENTRIES)
GAP = 2
PIECE = 64
GROUP = 256


def source_of(link, dx, dy, v):
    if link == 0:
        return (dx + 3) % 4, dy, v
    if link == 1:
        return (dx + 1) % 4, dy, v
    if link < 4:
        return dx, 1 - dy, v
    return dx, dy, v ^ 1


def group_plan():
    done = {}
    for t, _, dx, dy, v in ENTRIES:
        key = (dx, dy, v // 4)
        done[key] = max(done.get(key, 0), t)
    return done


GROUP_DONE = group_plan()


def lookup(index, values):
    out = jnp.int32(values[0])
    for i in range(1, len(values)):
        out = jnp.where(index == i, jnp.int32(values[i]), out)
    return out


def kernel(
    len_ref, assign_ref, adv_ref, hid_ref, gain_ref, w_ref, bias_ref, ad_ref, up_ref, og_ref,
    att_out, down_out, up_out,
    hbuf, nbuf, mnorm, wbuf, adbuf, ogbuf, acc, ssq, qbuf, kbuf, vbuf, low2, attb, pbuf, qg, lg,
    flags, pay_s, rec_s, pay_a, rec_a, pay_b, rec_b, pay_c, rec_c,
    hsem, lsem, wsend, wrecv, csend, crecv, msem, fsem, frecv, ssem, srecv, asem, arecv, bsem,
    brecv, gsem, grecv,
):
    me_d, me_f = lax.axis_index("dp"), lax.axis_index("fsdp")
    z, yh = me_d // 2, me_d % 2
    yl, x, c = me_f // 8, (me_f // 2) % 4, me_f % 2
    y = yh * 2 + yl
    par = z % 2
    chip = me_f // 2
    mate_f = me_f + 1 - 2 * c
    mate = (me_d, mate_f)

    def at(z_, y_, x_):
        return ((z_ % 8) * 2 + (y_ % 4) // 2, ((y_ % 4) % 2) * 8 + (x_ % 4) * 2 + c)

    receivers = (
        at(z, y, x + 3), at(z, y, x + 1), at(z, y + 3, x), at(z, y + 1, x), at(z + 7, y, x), at(z + 1, y, x),
    )
    cross = at(z, y + 1 - 2 * (1 - yl) + 4, x)
    f_peers = [(me_d, (me_f + k) % 16) for k in range(1, 16)]
    d_peers = [((me_d + k) % 16, me_f) for k in range(1, 16)]

    barrier = pltpu.get_barrier_semaphore()
    for peer in f_peers + d_peers + [cross]:
        pl.semaphore_signal(barrier, inc=1, device_id=peer, device_id_type=MESH)

    def hidden_copy(g):
        return pltpu.make_async_copy(
            hid_ref.at[:, pl.ds(pl.multiple_of(g * GROUP, GROUP), GROUP)], hbuf.at[g], hsem.at[g]
        )

    def start_hidden(g, carry):
        hidden_copy(g).start()
        return carry

    lax.fori_loop(0, 32, start_hidden, 0)
    local = [
        pltpu.make_async_copy(w_ref, wbuf.at[me_f], lsem.at[0]),
        pltpu.make_async_copy(ad_ref, adbuf, lsem.at[1]),
        pltpu.make_async_copy(og_ref, ogbuf, lsem.at[2]),
    ]
    for copy in local:
        copy.start()
    ssq[...] = jnp.zeros_like(ssq)
    for r in range(8):
        flags[me_d, pl.ds(r, 1), :] = jnp.full((1, 128), assign_ref[r], jnp.int32)

    pl.semaphore_wait(barrier, 31)

    def shard(dx, dy, core):
        yy = yl + dy - 2 * yl * dy
        return yy * 8 + ((x + dx) % 4) * 2 + core

    def rows_of(v):
        k = v + par if v % 2 == 0 else v - par
        return pl.ds(pl.multiple_of(k * PIECE, PIECE), PIECE)

    def piece_send(e):
        _, link, dx, dy, v = ENTRIES[e]
        sx, sy, sv = source_of(link, dx, dy, v)
        f, rows = shard(sx, sy, c), rows_of(sv)
        own = (sx, sy) == (0, 0)
        return pltpu.make_async_remote_copy(
            src_ref=w_ref.at[rows] if own else wbuf.at[f, rows],
            dst_ref=wbuf.at[f, rows],
            send_sem=wsend.at[e], recv_sem=wrecv.at[e],
            device_id=receivers[link], device_id_type=MESH,
        )

    def piece_landing(e):
        _, link, dx, dy, v = ENTRIES[e]
        spot = wbuf.at[shard(dx, dy, c), rows_of(v)]
        return pltpu.make_async_remote_copy(
            src_ref=spot, dst_ref=spot, send_sem=wsend.at[e], recv_sem=wrecv.at[e],
            device_id=mate, device_id_type=MESH,
        )

    def core_send(dx, dy, h):
        i = (dx * 2 + dy) * 2 + h
        f = shard(dx, dy, c)
        rows = pl.ds(h * GROUP, GROUP)
        own = (dx, dy) == (0, 0)
        return pltpu.make_async_remote_copy(
            src_ref=w_ref.at[rows] if own else wbuf.at[f, rows],
            dst_ref=wbuf.at[f, rows],
            send_sem=csend.at[i], recv_sem=crecv.at[i],
            device_id=mate, device_id_type=MESH,
        )

    def core_landing(dx, dy, h):
        i = (dx * 2 + dy) * 2 + h
        spot = wbuf.at[shard(dx, dy, 1 - c), pl.ds(h * GROUP, GROUP)]
        return pltpu.make_async_remote_copy(
            src_ref=spot, dst_ref=spot, send_sem=csend.at[i], recv_sem=crecv.at[i],
            device_id=mate, device_id_type=MESH,
        )

    def multiply(items):
        fx = [i[0] for i in items]
        fy = [i[1] for i in items]
        fh = [i[2] for i in items]
        fm = [i[3] for i in items]

        def body(i, carry):
            mine = lookup(i, fm)
            f = shard(lookup(i, fx), lookup(i, fy), c * mine + (1 - c) * (1 - mine))
            h = lookup(i, fh)
            rows = pl.ds(pl.multiple_of(h * GROUP, GROUP), GROUP)
            acc[...] += jnp.dot(nbuf[f * 2 + h], wbuf[f, rows, :], preferred_element_type=jnp.float32)
            return carry

        lax.fori_loop(0, len(items), body, 0)

    def sum_squares(g, carry):
        hidden_copy(g).wait()
        wide = hbuf[g].astype(jnp.float32)
        squared = wide * wide
        ssq[...] += squared[:, :128] + squared[:, 128:]
        return carry

    def scale_group(g, carry):
        gain = gain_ref[:, pl.ds(pl.multiple_of(g * GROUP, GROUP), GROUP)]
        nbuf[g] = (hbuf[g].astype(jnp.float32) * ssq[:, :1] * gain).astype(jnp.bfloat16)
        return carry

    def lora_group(g, carry):
        low2[...] += jnp.dot(nbuf[g], adbuf[g], preferred_element_type=jnp.float32)
        return carry

    flag_copies = [
        pltpu.make_async_remote_copy(
            src_ref=flags.at[me_d], dst_ref=flags.at[me_d], send_sem=fsem.at[k], recv_sem=frecv.at[k],
            device_id=d_peers[k], device_id_type=MESH,
        )
        for k in range(15)
    ]
    norm_copies = [
        pltpu.make_async_remote_copy(
            src_ref=nbuf.at[2 * d + 1 - c], dst_ref=mnorm.at[d], send_sem=msem.at[0, d], recv_sem=msem.at[1, d],
            device_id=mate, device_id_type=MESH,
        )
        for d in range(16)
    ]

    by_step = [[e for e in range(N_ENTRIES) if ENTRIES[e][0] == t] for t in range(len(SCHEDULE))]
    ready = [(0, 0, 0, 1), (0, 0, 1, 1)]
    mates = {0: [(0, 0, 0), (0, 0, 1)]}
    n_steps = len(SCHEDULE) + GAP
    bias_row = bias_ref[...].astype(jnp.float32)
    acc[...] = jnp.broadcast_to(bias_row, acc.shape)
    low2[...] = jnp.zeros_like(low2)
    for t in range(n_steps):
        if t >= GAP:
            for e in by_step[t - GAP]:
                piece_landing(e).wait_recv()
        if t < len(SCHEDULE):
            for e in by_step[t]:
                piece_send(e).start()
        if t == 0:
            core_send(0, 0, 0).start()
            core_send(0, 0, 1).start()
        for key, done in GROUP_DONE.items():
            if done == t - GAP:
                core_send(*key).start()
                ready.append(key + (1,))
                mates.setdefault(t, []).append(key)
        if t == 1:
            for copy in flag_copies:
                copy.start()
            lax.fori_loop(0, 32, sum_squares, 0)
            mean = jnp.sum(ssq[...], axis=1, keepdims=True) * (1.0 / 8192.0)
            ssq[...] = jnp.broadcast_to(lax.rsqrt(mean + EPSILON), ssq.shape)
        if t == 2:
            lax.fori_loop(0, 16, scale_group, 0)
        if t == 3:
            lax.fori_loop(16, 32, scale_group, 0)
            for copy in norm_copies:
                copy.start()
        if t == 4:
            local[1].wait()
            lax.fori_loop(0, 32, lora_group, 0)
            local[0].wait()
        if t >= 5:
            for s in [s for s in mates if s < t]:
                for key in mates.pop(s):
                    core_landing(*key).wait_recv()
                    ready.append(key + (0,))
            if ready:
                multiply(ready)
                ready = []
    last = [key for s in mates for key in mates[s]]
    for key in last:
        core_landing(*key).wait_recv()
    if last:
        multiply([key + (0,) for key in last])

    low = low2[...].astype(jnp.bfloat16)
    low_wide = jnp.concatenate([low, low], axis=1)
    lora = jnp.dot(low, up_ref[...], preferred_element_type=jnp.float32)
    qbuf[...] = (acc[:, :512] + ADAPTER_SCALE * lora).astype(jnp.bfloat16)
    kbuf[...] = acc[:, 512:640].astype(jnp.bfloat16)
    vbuf[...] = acc[:, 640:].astype(jnp.bfloat16)
    row = lax.broadcasted_iota(jnp.int32, (128, 128), 0)
    col = lax.broadcasted_iota(jnp.int32, (128, 128), 1)
    same = (row // 32) == (col // 32)
    causal = same & ((col % 32) <= (row % 32))
    scale = 128 ** (-0.5)

    def spread(ref, half, where, kind):
        out = jnp.full((128, 128), ref[half * 4].astype(kind), kind)
        for r in range(1, 4):
            out = jnp.where(where // 32 == r, jnp.full((128, 128), ref[half * 4 + r].astype(kind), kind), out)
        return out

    lives = []
    for half in range(2):
        rows = slice(half * 128, half * 128 + 128)
        visible = causal & ((col % 32) < spread(len_ref, half, col, jnp.int32))
        live = (row % 32) < spread(len_ref, half, row, jnp.int32)
        lives.append(live)
        for h in range(4):
            cols = slice(h * 128, h * 128 + 128)
            scores = lax.dot_general(qbuf[rows, cols], kbuf[rows, :], NT, preferred_element_type=jnp.float32)
            scores = jnp.where(visible, scores * scale, jnp.float32(-1e30))
            raised = jnp.exp(scores - jnp.max(scores, axis=-1, keepdims=True))
            soft = raised / jnp.sum(raised, axis=-1, keepdims=True)
            pbuf[half * 4 + h] = soft
            out = jnp.dot(soft.astype(jnp.bfloat16), vbuf[rows, :], preferred_element_type=jnp.float32)
            out = jnp.where(live, out, 0.0).astype(jnp.bfloat16)
            attb[half * 4 : half * 4 + 4, :, cols] = out.reshape(4, 32, 128)

    def fill_slot(d, carry):
        which = jnp.int32(0)
        for r in range(1, 8):
            which = jnp.where(assign_ref[r] == d, jnp.int32(r), which)
        pay_s[d] = attb[which]
        return carry

    lax.fori_loop(0, 16, fill_slot, 0)
    rec_s[me_d] = pay_s[me_d]
    slot_copies = [
        pltpu.make_async_remote_copy(
            src_ref=pay_s.at[d_peers[k][0]], dst_ref=rec_s.at[me_d], send_sem=ssem.at[k], recv_sem=srecv.at[k],
            device_id=d_peers[k], device_id_type=MESH,
        )
        for k in range(15)
    ]
    for copy in slot_copies:
        copy.start()

    local[2].wait()
    for half in range(2):
        rows = slice(half * 128, half * 128 + 128)
        factor = spread(adv_ref, half, row, jnp.float32) / spread(len_ref, half, row, jnp.float32)
        for h in range(4):
            cols = slice(h * 128, h * 128 + 128)
            weighted = (ogbuf[rows, cols].astype(jnp.float32) * factor).astype(jnp.bfloat16)
            weighted = jnp.where(lives[half], weighted.astype(jnp.float32), 0.0).astype(jnp.bfloat16)
            dsoft = lax.dot_general(weighted, vbuf[rows, :], NT, preferred_element_type=jnp.float32)
            dsoft = dsoft.astype(jnp.bfloat16).astype(jnp.float32)
            soft = pbuf[half * 4 + h]
            inner = jnp.sum(dsoft * soft, axis=-1, keepdims=True)
            dscores = (soft * (dsoft - inner) * scale).astype(jnp.bfloat16)
            dquery = jnp.dot(dscores, kbuf[rows, :], preferred_element_type=jnp.float32)
            qg[rows, cols] = dquery.astype(jnp.bfloat16)
    low_grad = ADAPTER_SCALE * lax.dot_general(up_ref[...], qg[...], NT, preferred_element_type=jnp.float32)
    lg[0] = low_grad.astype(jnp.bfloat16)
    lg_copy = pltpu.make_async_remote_copy(
        src_ref=lg.at[0], dst_ref=lg.at[1], send_sem=msem.at[0, 16], recv_sem=msem.at[1, 16],
        device_id=mate, device_id_type=MESH,
    )
    lg_copy.start()
    up_grad = ADAPTER_SCALE * lax.dot_general(qg[...], low_wide, TN, preferred_element_type=jnp.float32)
    up_four = up_grad.reshape(16, 2, 16, 128)
    lane = lax.broadcasted_iota(jnp.int32, (16, 16, 128), 2)
    pay_b[:, 1] = jnp.where(lane < 64, up_four[:, 0], up_four[:, 1]).astype(jnp.bfloat16)
    for copy in norm_copies:
        copy.wait()
    lg_copy.wait()

    def down_slice(d, carry):
        part = jnp.dot(lg[0], nbuf[2 * d + c], preferred_element_type=jnp.float32)
        part += jnp.dot(lg[1], mnorm[d], preferred_element_type=jnp.float32)
        part = part.astype(jnp.bfloat16)
        for i in range(4):
            for j in range(2):
                pay_a[j * 4 + i, d] = part[i * 16 : i * 16 + 16, j * 128 : j * 128 + 128]
        return carry

    lax.fori_loop(0, 16, down_slice, 0)
    a_copies = [
        pltpu.make_async_remote_copy(
            src_ref=pay_a.at[(chip + k) % 8], dst_ref=rec_a.at[k - 1], send_sem=asem.at[k - 1],
            recv_sem=arecv.at[k - 1], device_id=(me_d, ((chip + k) % 8) * 2 + c), device_id_type=MESH,
        )
        for k in range(1, 8)
    ]
    for copy in a_copies:
        copy.start()
    for e in range(N_ENTRIES):
        piece_send(e).wait_send()
    for key in [(0, 0, 0), (0, 0, 1)] + list(GROUP_DONE):
        core_send(*key).wait_send()
    for copy in flag_copies:
        copy.wait()
    for copy in a_copies:
        copy.wait()
    total = pay_a[chip].astype(jnp.float32)
    for k in range(7):
        total += rec_a[k].astype(jnp.float32)
    pay_b[:, 0] = total.astype(jnp.bfloat16)
    b_copies = [
        pltpu.make_async_remote_copy(
            src_ref=pay_b.at[d_peers[k][0]], dst_ref=rec_b.at[k], send_sem=bsem.at[k], recv_sem=brecv.at[k],
            device_id=d_peers[k], device_id_type=MESH,
        )
        for k in range(15)
    ]
    for copy in b_copies:
        copy.start()

    for copy in slot_copies:
        copy.wait()
    held = [jnp.sum((flags[s] == me_d).astype(jnp.float32), axis=0, keepdims=True) for s in range(16)]
    before = [jnp.zeros((1, 128), jnp.float32)]
    for s in range(15):
        before.append(before[-1] + held[s])
    for i in range(8):
        picked = jnp.zeros((32, 512), jnp.bfloat16)
        for s in range(i, i + 9):
            take = jnp.where(before[s] == float(i), held[s], 0.0).astype(jnp.bfloat16)
            picked += rec_s[s] * jnp.concatenate([take] * 4, axis=1)
        att_out[i] = picked

    for copy in b_copies:
        copy.wait()
    total = pay_b[me_d].astype(jnp.float32)
    for k in range(15):
        total += rec_b[k].astype(jnp.float32)
    pay_c[...] = total
    rec_c[me_f] = total
    c_copies = [
        pltpu.make_async_remote_copy(
            src_ref=pay_c, dst_ref=rec_c.at[me_f], send_sem=gsem.at[k], recv_sem=grecv.at[k],
            device_id=f_peers[k], device_id_type=MESH,
        )
        for k in range(15)
    ]
    for copy in c_copies:
        copy.start()
    for copy in c_copies:
        copy.wait()
    for f in range(16):
        j, i, core = f // 8, (f // 2) % 4, f % 2
        down_out[i * 16 : i * 16 + 16, core * 256 + j * 128 : core * 256 + j * 128 + 128] = rec_c[f, 0]
    total = rec_c[0, 1]
    for f in range(1, 16):
        total += rec_c[f, 1]
    up_out[...] = total


def on_device(
    hidden_input, input_norm_gain, joined_weight, joined_bias, adapter_down, adapter_up, advantage,
    output_gradient, lengths, assignment,
):
    bf16, f32 = jnp.bfloat16, jnp.float32
    dma = pltpu.SemaphoreType.DMA
    smem = pl.BlockSpec(memory_space=pltpu.SMEM)
    vmem = pl.BlockSpec(memory_space=pltpu.VMEM)
    hbm = pl.BlockSpec(memory_space=pl.ANY)
    att, down, up = pl.pallas_call(
        kernel,
        out_shape=(
            jax.ShapeDtypeStruct((8, 32, 512), bf16),
            jax.ShapeDtypeStruct((64, 512), f32),
            jax.ShapeDtypeStruct((16, 128), f32),
        ),
        in_specs=[smem, smem, smem, hbm, vmem, hbm, vmem, hbm, vmem, hbm],
        out_specs=(vmem, vmem, vmem),
        scratch_shapes=[
            pltpu.VMEM((32, 256, 256), bf16),
            pltpu.VMEM((32, 256, 256), bf16),
            pltpu.VMEM((16, 256, 256), bf16),
            pltpu.VMEM((16, 512, 768), bf16),
            pltpu.VMEM((32, 256, 64), bf16),
            pltpu.VMEM((256, 512), bf16),
            pltpu.VMEM((256, 768), f32),
            pltpu.VMEM((256, 128), f32),
            pltpu.VMEM((256, 512), bf16),
            pltpu.VMEM((256, 128), bf16),
            pltpu.VMEM((256, 128), bf16),
            pltpu.VMEM((256, 64), f32),
            pltpu.VMEM((8, 32, 512), bf16),
            pltpu.VMEM((8, 128, 128), f32),
            pltpu.VMEM((256, 512), bf16),
            pltpu.VMEM((2, 64, 256), bf16),
            pltpu.VMEM((16, 8, 128), jnp.int32),
            pltpu.VMEM((16, 32, 512), bf16),
            pltpu.VMEM((16, 32, 512), bf16),
            pltpu.VMEM((8, 16, 16, 128), bf16),
            pltpu.VMEM((7, 16, 16, 128), bf16),
            pltpu.VMEM((16, 2, 16, 128), bf16),
            pltpu.VMEM((15, 2, 16, 128), bf16),
            pltpu.VMEM((2, 16, 128), f32),
            pltpu.VMEM((16, 2, 16, 128), f32),
            dma((32,)), dma((3,)), dma((N_ENTRIES,)), dma((N_ENTRIES,)), dma((16,)), dma((16,)),
            dma((2, 17)), dma((15,)), dma((15,)), dma((15,)), dma((15,)), dma((7,)), dma((7,)),
            dma((15,)), dma((15,)), dma((15,)), dma((15,)),
        ],
        compiler_params=pltpu.CompilerParams(
            collective_id=0, has_side_effects=True, vmem_limit_bytes=56 * 2**20
        ),
        name="block",
    )(
        lengths,
        assignment,
        advantage,
        hidden_input.reshape(256, 8192),
        input_norm_gain.reshape(1, 8192),
        joined_weight,
        joined_bias.reshape(1, 768),
        adapter_down.reshape(32, 256, 64),
        adapter_up,
        output_gradient.reshape(256, 512),
    )
    return att, down.T, up.reshape(16, 2, 64).transpose(2, 1, 0).reshape(64, 32)


def solution(mesh):
    in_specs = (
        P(("dp", "fsdp"), None, None),
        P(),
        P("fsdp", None),
        P(),
        P(),
        P(),
        P(("dp", "fsdp")),
        P(("dp", "fsdp"), None, None),
        P(("dp", "fsdp")),
        P(("dp", "fsdp")),
    )
    out_specs = (P(("dp", "fsdp"), None, None), P("dp", None), P(None, "dp"))
    return jax.shard_map(
        on_device, mesh=mesh, in_specs=in_specs, out_specs=out_specs, check_vma=False
    )
```

time: 639 us -> 91.2 us (0.14)
  waiting for transfers between devices: 521 us -> 0 us
  Pallas kernels: 0 us -> 81.7 us
  blocking collectives: 54.4 us -> 0 us
  matrix products: 19.1 us -> 0 us
  starting transfers between devices: 13.4 us -> 0 us
  between operations: 14 us -> 0.64 us
  other arithmetic: 9.16 us -> 0 us
    reduce_scatter x2 -> x0, waiting for transfers between devices: 321 us -> none  [the longest x1 169 us: on_device(): lax.psum_scatter(column_b, 'dp', scatter_dimension=1, tiled=True)]
    psum x1 -> x0, waiting for transfers between devices: 124 us -> none  [on_device(): column_a, column_b = lax.psum((down_gradient, up_gradient), 'fsdp')]
    pallas_call x0 -> x1, Pallas kernels: none -> 81.7 us  [on_device(): pl.pallas_call(kernel, out_shape=(jax.ShapeDtypeStruct((8, 32, 512), bf16...]
    all_gather x1 -> x0, waiting for transfers between devices: 70.2 us -> none  [on_device(): lax.all_gather(joined_weight, 'fsdp', axis=0, tiled=True)]
    psum x1 -> x0, blocking collectives: 54.4 us -> none  [on_device(): column_a, column_b = lax.psum((down_gradient, up_gradient), 'fsdp')]
    dot_general x11 -> x0, matrix products: 19.1 us -> none  [the longest x1 8.84 us: on_device(): jnp.dot(normalized_rows, lax.all_gather(joined_weight, 'fsdp', axis=0, ti...]
    all_to_all x2 -> x0, starting transfers between devices: 13.2 us -> none  [the longest x1 9.15 us: on_device(): lax.all_to_all(sent, 'dp', split_axis=0, concat_axis=0, tiled=True) > 0]
  transfers between devices with their start and end apart: 6 -> 0, of which waited for: 5 -> 0; matrix products, arithmetic and copies ran while one was open for 3% -> 0% of each run, Pallas kernels for 0% -> 0%
where the time goes in v2:
time: 91.2 us; the launch traced here: 91 us
  Pallas kernels  81.7 us (90%)
  local copies, waits for them, and re-layouts  8.66 us (9%)
    pallas_call x1, Pallas kernels, on_device(): pl.pallas_call(kernel, out_shape=(jax.ShapeDtypeStruct((8, 32, 512), bf16...  81.7 us
    unnamed x3, local copies, waits for them, and re-layouts  6.01 us

profile of v2, /device:TPU:1, one launch (start us, length us, event | category | flops | bytes accessed | tf_op | source)
XLA Modules:
  0.0 91.0 jit_solution(11154941484678257300)
XLA Ops:
  0.6 1.3 %reshape.29.bias_ref = bf16[1,768]{1,0:T(2,128)(2,1)} reshape(bf16[768]{0:T(1024)(128)(2,1)} %param.13) | data formatting | bytes 3072 | tf_op jit(solution)/shard_map/reshape | solution.py:488
  1.9 2.8 %copy.13 = bf16[8192,64]{1,0:T(8,128)(2,1)} copy(bf16[8192,64]{0,1:T(8,128)(2,1)} %param.14) | data formatting | bytes 2097152 | tf_op args[4]
  4.7 81.7 %block.1 = (bf16[8,32,512]{2,1,0:T(8,128)(2,1)}, f32[64,512]{1,0:T(8,128)}, f32[16,128]{1,0:T(8,128)}) custom-call(s32[8]{0:T(128)} %len_ref.1, s32[8]{0:T(128)} %assign_ref.1, f32[8]{0:T(128)} %adv_ref.1, bf16[256,8192]{1,0:T(8,128)(2,1)} %bitcast.8, f32[1,8192]{1,0:T(1,128)} %bitcast.12, bf16[512,768]{1,0:T(8,128)(2,1)} %w_ref.1, ...), custom_call_target="tpu_custom_call" | custom-call | tf_op jit(solution)/shard_map/block/pallas_call | solution.py:438
  86.3 0.8 reshape.32
  87.1 0.6 copy.14
  87.7 1.7 %copy.17 = bf16[8,32,512]{2,1,0:T(8,128)(2,1)} copy(bf16[8,32,512]{2,1,0:T(8,128)(2,1)} %get-tuple-element.12) | data formatting | bytes 524288
  89.4 1.6 %copy.18 = f32[512,64]{0,1:T(8,128)} copy(f32[512,64]{0,1:T(8,128)} %bitcast.10) | data formatting | bytes 262144

commit v3 on v2

--- a/solution.py
+++ b/solution.py
@@ -1,5 +1,3 @@
-import functools
-
 import jax
 import jax.numpy as jnp
 from jax import lax
@@ -29,6 +27,8 @@
 N_ENTRIES = len(ENTRIES)
 GAP = 2
 PIECE = 64
+ORDER = (7, 8, 9, 10, 6, 5, 11, 12, 4, 3, 13, 14, 2, 1, 15, 0)
+CHUNK = 4
 GROUP = 256
 
 
@@ -61,11 +61,12 @@
 
 
 def kernel(
-    len_ref, assign_ref, adv_ref, hid_ref, gain_ref, w_ref, bias_ref, ad_ref, up_ref, og_ref,
-    att_out, down_out, up_out,
-    hbuf, nbuf, mnorm, wbuf, adbuf, ogbuf, acc, ssq, qbuf, kbuf, vbuf, low2, attb, pbuf, qg, lg,
-    flags, pay_s, rec_s, pay_a, rec_a, pay_b, rec_b, pay_c, rec_c,
-    hsem, lsem, wsend, wrecv, csend, crecv, msem, fsem, frecv, ssem, srecv, asem, arecv, bsem,
+    len_hbm, assign_hbm, adv_hbm, hid_ref, gain_hbm, w_ref, bias_hbm, ad_hbm, up_hbm, og_hbm,
+    att_out, rec_c,
+    len_ref, assign_ref, adv_ref, gain_ref, bias_ref, ad_ref, up_ref, og_ref,
+    hbuf, nbuf, mnorm, wbuf, acc, ssq, qbuf, kbuf, vbuf, low2, attb, pbuf, qg, lg,
+    flags, pay_s, rec_s, ordered, pay_a, rec_a, pay_b, rec_b, pay_c,
+    tokens, hsem, lsem, wsend, wrecv, csend, crecv, msem, fsem, frecv, ssem, srecv, asem, arecv, bsem,
     brecv, gsem, grecv,
 ):
     me_d, me_f = lax.axis_index("dp"), lax.axis_index("fsdp")
@@ -83,12 +84,12 @@
     receivers = (
         at(z, y, x + 3), at(z, y, x + 1), at(z, y + 3, x), at(z, y + 1, x), at(z + 7, y, x), at(z + 1, y, x),
     )
-    cross = at(z, y + 1 - 2 * (1 - yl) + 4, x)
+    neighbours = receivers + (mate,)
     f_peers = [(me_d, (me_f + k) % 16) for k in range(1, 16)]
     d_peers = [((me_d + k) % 16, me_f) for k in range(1, 16)]
 
     barrier = pltpu.get_barrier_semaphore()
-    for peer in f_peers + d_peers + [cross]:
+    for peer in neighbours:
         pl.semaphore_signal(barrier, inc=1, device_id=peer, device_id_type=MESH)
 
     def hidden_copy(g):
@@ -102,17 +103,25 @@
 
     lax.fori_loop(0, 32, start_hidden, 0)
     local = [
-        pltpu.make_async_copy(w_ref, wbuf.at[me_f], lsem.at[0]),
-        pltpu.make_async_copy(ad_ref, adbuf, lsem.at[1]),
-        pltpu.make_async_copy(og_ref, ogbuf, lsem.at[2]),
+        pltpu.make_async_copy(src, dst, lsem.at[i])
+        for i, (src, dst) in enumerate((
+            (w_ref, wbuf.at[me_f]), (ad_hbm, ad_ref), (og_hbm, og_ref), (len_hbm, len_ref), (assign_hbm, assign_ref),
+            (adv_hbm, adv_ref), (gain_hbm, gain_ref), (bias_hbm, bias_ref), (up_hbm, up_ref),
+        ))
     ]
     for copy in local:
         copy.start()
     ssq[...] = jnp.zeros_like(ssq)
-    for r in range(8):
-        flags[me_d, pl.ds(r, 1), :] = jnp.full((1, 128), assign_ref[r], jnp.int32)
-
-    pl.semaphore_wait(barrier, 31)
+    low2[...] = jnp.zeros_like(low2)
+
+    pl.semaphore_wait(barrier, 7)
+
+    def send_tokens(i):
+        for peer in neighbours:
+            pl.semaphore_signal(tokens.at[i], inc=1, device_id=peer, device_id_type=MESH)
+
+    def take_tokens(i):
+        pl.semaphore_wait(tokens.at[i], 7)
 
     def shard(dx, dy, core):
         yy = yl + dy - 2 * yl * dy
@@ -191,7 +200,8 @@
         return carry
 
     def lora_group(g, carry):
-        low2[...] += jnp.dot(nbuf[g], adbuf[g], preferred_element_type=jnp.float32)
+        cols = pl.ds(pl.multiple_of(g * GROUP, GROUP), GROUP)
+        low2[...] += lax.dot_general(nbuf[g], ad_ref[:, cols], NT, preferred_element_type=jnp.float32)
         return carry
 
     flag_copies = [
@@ -213,9 +223,6 @@
     ready = [(0, 0, 0, 1), (0, 0, 1, 1)]
     mates = {0: [(0, 0, 0), (0, 0, 1)]}
     n_steps = len(SCHEDULE) + GAP
-    bias_row = bias_ref[...].astype(jnp.float32)
-    acc[...] = jnp.broadcast_to(bias_row, acc.shape)
-    low2[...] = jnp.zeros_like(low2)
     for t in range(n_steps):
         if t >= GAP:
             for e in by_step[t - GAP]:
@@ -223,6 +230,10 @@
         if t < len(SCHEDULE):
             for e in by_step[t]:
                 piece_send(e).start()
+        if 1 <= t <= 5:
+            take_tokens(t - 1)
+        if t < 5:
+            send_tokens(t)
         if t == 0:
             core_send(0, 0, 0).start()
             core_send(0, 0, 1).start()
@@ -232,12 +243,11 @@
                 ready.append(key + (1,))
                 mates.setdefault(t, []).append(key)
         if t == 1:
-            for copy in flag_copies:
-                copy.start()
             lax.fori_loop(0, 32, sum_squares, 0)
             mean = jnp.sum(ssq[...], axis=1, keepdims=True) * (1.0 / 8192.0)
             ssq[...] = jnp.broadcast_to(lax.rsqrt(mean + EPSILON), ssq.shape)
         if t == 2:
+            local[6].wait()
             lax.fori_loop(0, 16, scale_group, 0)
         if t == 3:
             lax.fori_loop(16, 32, scale_group, 0)
@@ -247,6 +257,15 @@
             local[1].wait()
             lax.fori_loop(0, 32, lora_group, 0)
             local[0].wait()
+            local[7].wait()
+            acc[...] = jnp.broadcast_to(bias_ref[...].astype(jnp.float32).reshape(1, 768), acc.shape)
+        if t == 6:
+            for i in (3, 4, 5, 8):
+                local[i].wait()
+            for r in range(8):
+                flags[me_d, pl.ds(r, 1), :] = jnp.full((1, 128), assign_ref[r], jnp.int32)
+            for copy in flag_copies:
+                copy.start()
         if t >= 5:
             for s in [s for s in mates if s < t]:
                 for key in mates.pop(s):
@@ -321,7 +340,7 @@
         factor = spread(adv_ref, half, row, jnp.float32) / spread(len_ref, half, row, jnp.float32)
         for h in range(4):
             cols = slice(h * 128, h * 128 + 128)
-            weighted = (ogbuf[rows, cols].astype(jnp.float32) * factor).astype(jnp.bfloat16)
+            weighted = (og_ref[rows, cols].astype(jnp.float32) * factor).astype(jnp.bfloat16)
             weighted = jnp.where(lives[half], weighted.astype(jnp.float32), 0.0).astype(jnp.bfloat16)
             dsoft = lax.dot_general(weighted, vbuf[rows, :], NT, preferred_element_type=jnp.float32)
             dsoft = dsoft.astype(jnp.bfloat16).astype(jnp.float32)
@@ -340,51 +359,58 @@
     up_grad = ADAPTER_SCALE * lax.dot_general(qg[...], low_wide, TN, preferred_element_type=jnp.float32)
     up_four = up_grad.reshape(16, 2, 16, 128)
     lane = lax.broadcasted_iota(jnp.int32, (16, 16, 128), 2)
-    pay_b[:, 1] = jnp.where(lane < 64, up_four[:, 0], up_four[:, 1]).astype(jnp.bfloat16)
+    ordered[...] = jnp.where(lane < 64, up_four[:, 0], up_four[:, 1]).astype(jnp.bfloat16)
     for copy in norm_copies:
         copy.wait()
     lg_copy.wait()
 
-    def down_slice(d, carry):
+    def down_slice(i, carry):
+        d = (me_d + lookup(i, ORDER)) % 16
         part = jnp.dot(lg[0], nbuf[2 * d + c], preferred_element_type=jnp.float32)
         part += jnp.dot(lg[1], mnorm[d], preferred_element_type=jnp.float32)
         part = part.astype(jnp.bfloat16)
-        for i in range(4):
-            for j in range(2):
-                pay_a[j * 4 + i, d] = part[i * 16 : i * 16 + 16, j * 128 : j * 128 + 128]
+        for i2 in range(4):
+            for j2 in range(2):
+                pay_a[j2 * 4 + i2, i] = part[i2 * 16 : i2 * 16 + 16, j2 * 128 : j2 * 128 + 128]
         return carry
 
-    lax.fori_loop(0, 16, down_slice, 0)
-    a_copies = [
-        pltpu.make_async_remote_copy(
-            src_ref=pay_a.at[(chip + k) % 8], dst_ref=rec_a.at[k - 1], send_sem=asem.at[k - 1],
-            recv_sem=arecv.at[k - 1], device_id=(me_d, ((chip + k) % 8) * 2 + c), device_id_type=MESH,
-        )
-        for k in range(1, 8)
-    ]
-    for copy in a_copies:
-        copy.start()
+    def a_copy(q, k):
+        span = pl.ds(q * CHUNK, CHUNK)
+        return pltpu.make_async_remote_copy(
+            src_ref=pay_a.at[(chip + k) % 8, span], dst_ref=rec_a.at[k - 1, span], send_sem=asem.at[q, k - 1],
+            recv_sem=arecv.at[q, k - 1], device_id=(me_d, ((chip + k) % 8) * 2 + c), device_id_type=MESH,
+        )
+
+    chunks = range(16 // CHUNK)
+    for q in chunks:
+        lax.fori_loop(q * CHUNK, (q + 1) * CHUNK, down_slice, 0)
+        for k in range(1, 8):
+            a_copy(q, k).start()
     for e in range(N_ENTRIES):
         piece_send(e).wait_send()
     for key in [(0, 0, 0), (0, 0, 1)] + list(GROUP_DONE):
         core_send(*key).wait_send()
     for copy in flag_copies:
         copy.wait()
-    for copy in a_copies:
-        copy.wait()
-    total = pay_a[chip].astype(jnp.float32)
-    for k in range(7):
-        total += rec_a[k].astype(jnp.float32)
-    pay_b[:, 0] = total.astype(jnp.bfloat16)
     b_copies = [
         pltpu.make_async_remote_copy(
-            src_ref=pay_b.at[d_peers[k][0]], dst_ref=rec_b.at[k], send_sem=bsem.at[k], recv_sem=brecv.at[k],
-            device_id=d_peers[k], device_id_type=MESH,
-        )
-        for k in range(15)
+            src_ref=pay_b.at[i], dst_ref=rec_b.at[i], send_sem=bsem.at[i], recv_sem=brecv.at[i],
+            device_id=((me_d + ORDER[i]) % 16, me_f), device_id_type=MESH,
+        )
+        for i in range(15)
     ]
-    for copy in b_copies:
-        copy.start()
+    for q in chunks:
+        span = pl.ds(q * CHUNK, CHUNK)
+        for k in range(1, 8):
+            a_copy(q, k).wait()
+        total = pay_a[chip, span].astype(jnp.float32)
+        for k in range(7):
+            total += rec_a[k, span].astype(jnp.float32)
+        pay_b[span, 0] = total.astype(jnp.bfloat16)
+        for i in range(q * CHUNK, (q + 1) * CHUNK):
+            pay_b[i, 1] = ordered[(me_d + ORDER[i]) % 16]
+            if i < 15:
+                b_copies[i].start()
 
     for copy in slot_copies:
         copy.wait()
@@ -397,15 +423,16 @@
         for s in range(i, i + 9):
             take = jnp.where(before[s] == float(i), held[s], 0.0).astype(jnp.bfloat16)
             picked += rec_s[s] * jnp.concatenate([take] * 4, axis=1)
-        att_out[i] = picked
+        attb[i] = picked
+    att_copy = pltpu.make_async_copy(attb, att_out, lsem.at[9])
+    att_copy.start()
 
     for copy in b_copies:
         copy.wait()
-    total = pay_b[me_d].astype(jnp.float32)
+    total = pay_b[15].astype(jnp.float32)
     for k in range(15):
         total += rec_b[k].astype(jnp.float32)
-    pay_c[...] = total
-    rec_c[me_f] = total
+    pay_c[...] = total.astype(jnp.bfloat16)
     c_copies = [
         pltpu.make_async_remote_copy(
             src_ref=pay_c, dst_ref=rec_c.at[me_f], send_sem=gsem.at[k], recv_sem=grecv.at[k],
@@ -415,15 +442,26 @@
     ]
     for copy in c_copies:
         copy.start()
+    own_copy = pltpu.make_async_copy(pay_c, rec_c.at[me_f], lsem.at[10])
+    own_copy.start()
     for copy in c_copies:
         copy.wait()
+    own_copy.wait()
+    att_copy.wait()
+
+
+def assemble(att_ref, sums_ref, att_out, down_out, up_out):
+    att_out[...] = att_ref[...]
     for f in range(16):
         j, i, core = f // 8, (f // 2) % 4, f % 2
-        down_out[i * 16 : i * 16 + 16, core * 256 + j * 128 : core * 256 + j * 128 + 128] = rec_c[f, 0]
-    total = rec_c[0, 1]
+        down_out[i * 16 : i * 16 + 16, core * 256 + j * 128 : core * 256 + j * 128 + 128] = sums_ref[f, 0].astype(
+            jnp.float32
+        )
+    total = sums_ref[0, 1].astype(jnp.float32)
     for f in range(1, 16):
-        total += rec_c[f, 1]
-    up_out[...] = total
+        total += sums_ref[f, 1].astype(jnp.float32)
+    up_out[:16, :] = total[:, :64]
+    up_out[16:, :] = total[:, 64:]
 
 
 def on_device(
@@ -432,25 +470,26 @@
 ):
     bf16, f32 = jnp.bfloat16, jnp.float32
     dma = pltpu.SemaphoreType.DMA
-    smem = pl.BlockSpec(memory_space=pltpu.SMEM)
     vmem = pl.BlockSpec(memory_space=pltpu.VMEM)
     hbm = pl.BlockSpec(memory_space=pl.ANY)
-    att, down, up = pl.pallas_call(
+    att, sums = pl.pallas_call(
         kernel,
-        out_shape=(
-            jax.ShapeDtypeStruct((8, 32, 512), bf16),
-            jax.ShapeDtypeStruct((64, 512), f32),
-            jax.ShapeDtypeStruct((16, 128), f32),
-        ),
-        in_specs=[smem, smem, smem, hbm, vmem, hbm, vmem, hbm, vmem, hbm],
-        out_specs=(vmem, vmem, vmem),
+        out_shape=(jax.ShapeDtypeStruct((8, 32, 512), bf16), jax.ShapeDtypeStruct((16, 2, 16, 128), bf16)),
+        in_specs=[hbm] * 10,
+        out_specs=(hbm, hbm),
         scratch_shapes=[
+            pltpu.SMEM((8,), jnp.int32),
+            pltpu.SMEM((8,), jnp.int32),
+            pltpu.SMEM((8,), f32),
+            pltpu.VMEM((1, 8192), f32),
+            pltpu.VMEM((768,), bf16),
+            pltpu.VMEM((64, 8192), bf16),
+            pltpu.VMEM((64, 512), bf16),
+            pltpu.VMEM((256, 512), bf16),
             pltpu.VMEM((32, 256, 256), bf16),
             pltpu.VMEM((32, 256, 256), bf16),
             pltpu.VMEM((16, 256, 256), bf16),
             pltpu.VMEM((16, 512, 768), bf16),
-            pltpu.VMEM((32, 256, 64), bf16),
-            pltpu.VMEM((256, 512), bf16),
             pltpu.VMEM((256, 768), f32),
             pltpu.VMEM((256, 128), f32),
             pltpu.VMEM((256, 512), bf16),
@@ -464,14 +503,15 @@
             pltpu.VMEM((16, 8, 128), jnp.int32),
             pltpu.VMEM((16, 32, 512), bf16),
             pltpu.VMEM((16, 32, 512), bf16),
+            pltpu.VMEM((16, 16, 128), bf16),
             pltpu.VMEM((8, 16, 16, 128), bf16),
             pltpu.VMEM((7, 16, 16, 128), bf16),
             pltpu.VMEM((16, 2, 16, 128), bf16),
             pltpu.VMEM((15, 2, 16, 128), bf16),
-            pltpu.VMEM((2, 16, 128), f32),
-            pltpu.VMEM((16, 2, 16, 128), f32),
-            dma((32,)), dma((3,)), dma((N_ENTRIES,)), dma((N_ENTRIES,)), dma((16,)), dma((16,)),
-            dma((2, 17)), dma((15,)), dma((15,)), dma((15,)), dma((15,)), dma((7,)), dma((7,)),
+            pltpu.VMEM((2, 16, 128), bf16),
+            pltpu.SemaphoreType.REGULAR((5,)),
+            dma((32,)), dma((11,)), dma((N_ENTRIES,)), dma((N_ENTRIES,)), dma((16,)), dma((16,)),
+            dma((2, 17)), dma((15,)), dma((15,)), dma((15,)), dma((15,)), dma((16 // CHUNK, 7)), dma((16 // CHUNK, 7)),
             dma((15,)), dma((15,)), dma((15,)), dma((15,)),
         ],
         compiler_params=pltpu.CompilerParams(
@@ -485,12 +525,23 @@
         hidden_input.reshape(256, 8192),
         input_norm_gain.reshape(1, 8192),
         joined_weight,
-        joined_bias.reshape(1, 768),
-        adapter_down.reshape(32, 256, 64),
+        joined_bias,
+        adapter_down.T,
         adapter_up,
         output_gradient.reshape(256, 512),
     )
-    return att, down.T, up.reshape(16, 2, 64).transpose(2, 1, 0).reshape(64, 32)
+    att, down, up = pl.pallas_call(
+        assemble,
+        out_shape=(
+            jax.ShapeDtypeStruct((8, 32, 512), bf16),
+            jax.ShapeDtypeStruct((64, 512), f32),
+            jax.ShapeDtypeStruct((32, 64), f32),
+        ),
+        in_specs=[vmem, vmem],
+        out_specs=(vmem, vmem, vmem),
+        name="assemble",
+    )(att, sums)
+    return att, down.T, up.T
 
 
 def solution(mesh):

time: 91.2 us -> 77.2 us (0.85)
  local copies, waits for them, and re-layouts: 8.66 us -> 0 us
  Pallas kernels: 81.7 us -> 76.5 us
    pallas_call x1, Pallas kernels: 81.7 us -> 74.7 us  [on_device(): pl.pallas_call(kernel, out_shape=(jax.ShapeDtypeStruct((8, 32, 512), bf16...]
    unnamed x3 -> x0, local copies, waits for them, and re-layouts: 6.01 us -> none
    reshape x2 -> x0, local copies, waits for them, and re-layouts: 2.04 us -> none  [the longest x1 1.26 us: on_device(): joined_bias.reshape(1, 768)]
    pallas_call x0 -> x1, Pallas kernels: none -> 1.75 us  [on_device(): pl.pallas_call(assemble, out_shape=(jax.ShapeDtypeStruct((8, 32, 512), bf...]
where the time goes in v3:
time: 77.2 us; the launch traced here: 77.1 us
  Pallas kernels  76.5 us (99%)
    pallas_call x1, Pallas kernels, on_device(): pl.pallas_call(kernel, out_shape=(jax.ShapeDtypeStruct((8, 32, 512), bf16...  74.7 us
    pallas_call x1, Pallas kernels, on_device(): pl.pallas_call(assemble, out_shape=(jax.ShapeDtypeStruct((8, 32, 512), bf...  1.75 us

profile of v3, /device:TPU:1, one launch (start us, length us, event | category | flops | bytes accessed | tf_op | source)
XLA Modules:
  0.0 77.1 jit_solution(14535346965005678100)
XLA Ops:
  0.6 74.7 %block.1 = (bf16[8,32,512]{2,1,0:T(8,128)(2,1)}, bf16[16,2,16,128]{3,2,1,0:T(8,128)(2,1)}) custom-call(s32[8]{0:T(128)} %len_hbm.1, s32[8]{0:T(128)} %assign_hbm.1, f32[8]{0:T(128)} %adv_hbm.1, bf16[256,8192]{1,0:T(8,128)(2,1)} %bitcast.6, f32[1,8192]{1,0:T(1,128)} %bitcast.9, bf16[512,768]{1,0:T(8,128)(2,1)} %w_ref.1, bf16[768]{0:T(1024)(128)(2,1)} %bias_hbm.1, ...), custom_call_target="tpu_custom_call" | custom-call | tf_op jit(solution)/shard_map/block/pallas_call | solution.py:475
  75.4 1.8 %assemble.1 = (bf16[8,32,512]{2,1,0:T(8,128)(2,1)}, f32[64,512]{1,0:T(8,128)}, f32[32,64]{1,0:T(8,128)}) custom-call(bf16[8,32,512]{2,1,0:T(8,128)(2,1)} %get-tuple-element.8.att_ref, bf16[16,2,16,128]{3,2,1,0:T(8,128)(2,1)} %get-tuple-element.9.sums_ref), custom_call_target="tpu_custom_call" | custom-call | tf_op jit(solution)/shard_map/assemble/pallas_call | solution.py:533

commit v4 on v3

--- a/solution.py
+++ b/solution.py
@@ -12,20 +12,21 @@
 TN = (((0,), (0,)), ((), ()))
 
 SCHEDULE = (
-    ((0, 1, 0, 2), (1, 3, 0, 6), (2, 0, 1, 0), (3, 0, 1, 4)),
-    ((0, 1, 0, 0), (1, 3, 0, 2), (2, 0, 1, 6), (3, 0, 1, 2)),
-    ((0, 1, 0, 4), (1, 3, 0, 4), (2, 0, 1, 3), (3, 1, 1, 2), (4, 0, 1, 1), (5, 3, 0, 7)),
-    ((0, 1, 0, 6), (1, 3, 0, 0), (2, 1, 1, 0), (3, 0, 1, 5), (4, 0, 1, 7), (5, 1, 0, 3)),
-    ((0, 1, 0, 7), (1, 3, 1, 0), (2, 1, 1, 4), (3, 3, 1, 2), (4, 3, 0, 5), (5, 1, 1, 3)),
-    ((0, 2, 0, 6), (1, 2, 0, 0), (2, 3, 1, 4), (3, 1, 1, 6), (4, 1, 0, 1), (5, 1, 1, 1)),
-    ((0, 1, 0, 5), (1, 2, 0, 2), (2, 3, 1, 7), (3, 3, 1, 6), (4, 3, 1, 1), (5, 1, 1, 5)),
-    ((0, 2, 1, 4), (1, 2, 0, 4), (2, 2, 1, 6), (3, 3, 1, 5), (4, 3, 1, 3), (5, 2, 0, 1)),
-    ((0, 2, 0, 5), (1, 3, 0, 3), (2, 1, 1, 7), (3, 3, 0, 1), (4, 2, 0, 7), (5, 2, 0, 3)),
-    ((0, 2, 1, 3), (1, 2, 1, 2), (2, 2, 1, 1), (3, 2, 1, 0), (4, 2, 1, 7), (5, 2, 1, 5)),
+    ((0, 1, 0, 4), (1, 3, 0, 0), (2, 0, 1, 4), (3, 0, 1, 6)),
+    ((0, 1, 0, 0), (1, 3, 0, 4), (2, 0, 1, 0), (3, 0, 1, 2)),
+    ((0, 1, 0, 2), (1, 3, 0, 6), (2, 0, 1, 5), (3, 0, 1, 1)),
+    ((0, 1, 1, 6), (1, 3, 0, 2), (2, 1, 1, 4), (3, 3, 1, 0), (4, 1, 0, 5), (5, 3, 0, 1)),
+    ((0, 1, 0, 6), (1, 3, 1, 2), (2, 1, 1, 0), (3, 0, 1, 7), (4, 1, 0, 1), (5, 3, 0, 5)),
+    ((0, 2, 0, 4), (1, 2, 0, 0), (2, 1, 1, 2), (3, 3, 1, 6), (4, 3, 0, 7), (5, 1, 0, 3)),
+    ((0, 2, 1, 4), (1, 2, 0, 2), (2, 0, 1, 3), (3, 3, 1, 4), (4, 3, 1, 1), (5, 1, 1, 7)),
+    ((0, 1, 0, 7), (1, 2, 0, 6), (2, 1, 1, 5), (3, 1, 1, 1), (4, 3, 0, 3), (5, 3, 1, 3)),
+    ((0, 2, 1, 6), (1, 2, 1, 2), (2, 3, 1, 7), (3, 2, 1, 0), (4, 2, 0, 5), (5, 2, 0, 1)),
+    ((0, 2, 1, 7), (1, 2, 0, 7), (2, 1, 1, 3), (3, 3, 1, 5), (4, 2, 0, 3), (5, 2, 1, 5)),
+    ((0, 2, 1, 1), (1, 2, 1, 3)),
 )
 ENTRIES = tuple((t,) + e for t, row in enumerate(SCHEDULE) for e in row)
 N_ENTRIES = len(ENTRIES)
-GAP = 2
+GAP = 3
 PIECE = 64
 ORDER = (7, 8, 9, 10, 6, 5, 11, 12, 4, 3, 13, 14, 2, 1, 15, 0)
 CHUNK = 4
@@ -51,6 +52,22 @@
 
 
 GROUP_DONE = group_plan()
+AHEAD = 1
+
+
+def issue_plan():
+    slot_of = {(dx, dy, v): t for t, _, dx, dy, v in ENTRIES}
+    plan = [[] for _ in range(len(SCHEDULE) + GAP)]
+    latest = {}
+    for e, (t, link, dx, dy, v) in enumerate(ENTRIES):
+        sx, sy, sv = source_of(link, dx, dy, v)
+        have = 0 if (sx, sy) == (0, 0) else slot_of[sx, sy, sv] + GAP
+        latest[link] = max(have, t - AHEAD, latest.get(link, 0))
+        plan[latest[link]].append(e)
+    return plan
+
+
+ISSUE = issue_plan()
 
 
 def lookup(index, values):
@@ -64,9 +81,9 @@
     len_hbm, assign_hbm, adv_hbm, hid_ref, gain_hbm, w_ref, bias_hbm, ad_hbm, up_hbm, og_hbm,
     att_out, rec_c,
     len_ref, assign_ref, adv_ref, gain_ref, bias_ref, ad_ref, up_ref, og_ref,
-    hbuf, nbuf, mnorm, wbuf, acc, ssq, qbuf, kbuf, vbuf, low2, attb, pbuf, qg, lg,
+    hbuf, nbuf, wbuf, acc, part_acc, ssq, kbuf, vbuf, low2, attb, pbuf, qg, lg,
     flags, pay_s, rec_s, ordered, pay_a, rec_a, pay_b, rec_b, pay_c,
-    tokens, hsem, lsem, wsend, wrecv, csend, crecv, msem, fsem, frecv, ssem, srecv, asem, arecv, bsem,
+    tokens, hsem, lsem, wsend, wrecv, msem, fsem, frecv, ssem, srecv, asem, arecv, bsem,
     brecv, gsem, grecv,
 ):
     me_d, me_f = lax.axis_index("dp"), lax.axis_index("fsdp")
@@ -105,7 +122,7 @@
     local = [
         pltpu.make_async_copy(src, dst, lsem.at[i])
         for i, (src, dst) in enumerate((
-            (w_ref, wbuf.at[me_f]), (ad_hbm, ad_ref), (og_hbm, og_ref), (len_hbm, len_ref), (assign_hbm, assign_ref),
+            (w_ref, wbuf.at[chip]), (ad_hbm, ad_ref), (og_hbm, og_ref), (len_hbm, len_ref), (assign_hbm, assign_ref),
             (adv_hbm, adv_ref), (gain_hbm, gain_ref), (bias_hbm, bias_ref), (up_hbm, up_ref),
         ))
     ]
@@ -123,9 +140,8 @@
     def take_tokens(i):
         pl.semaphore_wait(tokens.at[i], 7)
 
-    def shard(dx, dy, core):
-        yy = yl + dy - 2 * yl * dy
-        return yy * 8 + ((x + dx) % 4) * 2 + core
+    def shard(dx, dy):
+        return (yl + dy - 2 * yl * dy) * 4 + (x + dx) % 4
 
     def rows_of(v):
         k = v + par if v % 2 == 0 else v - par
@@ -134,7 +150,7 @@
     def piece_send(e):
         _, link, dx, dy, v = ENTRIES[e]
         sx, sy, sv = source_of(link, dx, dy, v)
-        f, rows = shard(sx, sy, c), rows_of(sv)
+        f, rows = shard(sx, sy), rows_of(sv)
         own = (sx, sy) == (0, 0)
         return pltpu.make_async_remote_copy(
             src_ref=w_ref.at[rows] if own else wbuf.at[f, rows],
@@ -145,44 +161,20 @@
 
     def piece_landing(e):
         _, link, dx, dy, v = ENTRIES[e]
-        spot = wbuf.at[shard(dx, dy, c), rows_of(v)]
+        spot = wbuf.at[shard(dx, dy), rows_of(v)]
         return pltpu.make_async_remote_copy(
             src_ref=spot, dst_ref=spot, send_sem=wsend.at[e], recv_sem=wrecv.at[e],
             device_id=mate, device_id_type=MESH,
         )
 
-    def core_send(dx, dy, h):
-        i = (dx * 2 + dy) * 2 + h
-        f = shard(dx, dy, c)
-        rows = pl.ds(h * GROUP, GROUP)
-        own = (dx, dy) == (0, 0)
-        return pltpu.make_async_remote_copy(
-            src_ref=w_ref.at[rows] if own else wbuf.at[f, rows],
-            dst_ref=wbuf.at[f, rows],
-            send_sem=csend.at[i], recv_sem=crecv.at[i],
-            device_id=mate, device_id_type=MESH,
-        )
-
-    def core_landing(dx, dy, h):
-        i = (dx * 2 + dy) * 2 + h
-        spot = wbuf.at[shard(dx, dy, 1 - c), pl.ds(h * GROUP, GROUP)]
-        return pltpu.make_async_remote_copy(
-            src_ref=spot, dst_ref=spot, send_sem=csend.at[i], recv_sem=crecv.at[i],
-            device_id=mate, device_id_type=MESH,
-        )
-
-    def multiply(items):
-        fx = [i[0] for i in items]
-        fy = [i[1] for i in items]
-        fh = [i[2] for i in items]
-        fm = [i[3] for i in items]
-
+    def multiply(items, rows):
         def body(i, carry):
-            mine = lookup(i, fm)
-            f = shard(lookup(i, fx), lookup(i, fy), c * mine + (1 - c) * (1 - mine))
-            h = lookup(i, fh)
-            rows = pl.ds(pl.multiple_of(h * GROUP, GROUP), GROUP)
-            acc[...] += jnp.dot(nbuf[f * 2 + h], wbuf[f, rows, :], preferred_element_type=jnp.float32)
+            j = shard(lookup(i, [item[0] for item in items]), lookup(i, [item[1] for item in items]))
+            h = lookup(i, [item[2] for item in items])
+            span = pl.ds(pl.multiple_of(h * GROUP, GROUP), GROUP)
+            acc[rows, :] += jnp.dot(
+                nbuf[(2 * j + c) * 2 + h, rows, :], wbuf[j, span, :], preferred_element_type=jnp.float32
+            )
             return carry
 
         lax.fori_loop(0, len(items), body, 0)
@@ -196,12 +188,12 @@
 
     def scale_group(g, carry):
         gain = gain_ref[:, pl.ds(pl.multiple_of(g * GROUP, GROUP), GROUP)]
-        nbuf[g] = (hbuf[g].astype(jnp.float32) * ssq[:, :1] * gain).astype(jnp.bfloat16)
+        nbuf[g, :256, :] = (hbuf[g].astype(jnp.float32) * ssq[:, :1] * gain).astype(jnp.bfloat16)
         return carry
 
     def lora_group(g, carry):
         cols = pl.ds(pl.multiple_of(g * GROUP, GROUP), GROUP)
-        low2[...] += lax.dot_general(nbuf[g], ad_ref[:, cols], NT, preferred_element_type=jnp.float32)
+        low2[...] += lax.dot_general(nbuf[g, :256, :], ad_ref[:, cols], NT, preferred_element_type=jnp.float32)
         return carry
 
     flag_copies = [
@@ -211,54 +203,66 @@
         )
         for k in range(15)
     ]
-    norm_copies = [
-        pltpu.make_async_remote_copy(
-            src_ref=nbuf.at[2 * d + 1 - c], dst_ref=mnorm.at[d], send_sem=msem.at[0, d], recv_sem=msem.at[1, d],
-            device_id=mate, device_id_type=MESH,
-        )
-        for d in range(16)
-    ]
+    def norm_copy(i):
+        if i < 8:
+            place = pl.ds((2 * i + 1 - c) * 2, 2)
+        else:
+            place = pl.ds((2 * (i - 8) + c) * 2 + 1 - c, 1)
+        return pltpu.make_async_remote_copy(
+            src_ref=nbuf.at[place, pl.ds(0, 256)], dst_ref=nbuf.at[place, pl.ds(256, 256)],
+            send_sem=msem.at[0, i], recv_sem=msem.at[1, i], device_id=mate, device_id_type=MESH,
+        )
+
+    def part_copy(half):
+        rows = pl.ds(half * 128, 128)
+        return pltpu.make_async_remote_copy(
+            src_ref=acc.at[pl.ds(256 + half * 128, 128)], dst_ref=part_acc.at[rows],
+            send_sem=msem.at[0, 17 + half], recv_sem=msem.at[1, 17 + half], device_id=mate, device_id_type=MESH,
+        )
 
     by_step = [[e for e in range(N_ENTRIES) if ENTRIES[e][0] == t] for t in range(len(SCHEDULE))]
-    ready = [(0, 0, 0, 1), (0, 0, 1, 1)]
-    mates = {0: [(0, 0, 0), (0, 0, 1)]}
+    ready = [(0, 0, 0), (0, 0, 1)]
+    mine, others = slice(0, 256), slice(256, 512)
     n_steps = len(SCHEDULE) + GAP
     for t in range(n_steps):
         if t >= GAP:
             for e in by_step[t - GAP]:
                 piece_landing(e).wait_recv()
-        if t < len(SCHEDULE):
-            for e in by_step[t]:
-                piece_send(e).start()
+        for e in ISSUE[t]:
+            piece_send(e).start()
         if 1 <= t <= 5:
             take_tokens(t - 1)
         if t < 5:
             send_tokens(t)
-        if t == 0:
-            core_send(0, 0, 0).start()
-            core_send(0, 0, 1).start()
         for key, done in GROUP_DONE.items():
             if done == t - GAP:
-                core_send(*key).start()
-                ready.append(key + (1,))
-                mates.setdefault(t, []).append(key)
+                ready.append(key)
+        if t == 0:
+            lax.fori_loop(0, 16, sum_squares, 0)
         if t == 1:
-            lax.fori_loop(0, 32, sum_squares, 0)
+            lax.fori_loop(16, 32, sum_squares, 0)
             mean = jnp.sum(ssq[...], axis=1, keepdims=True) * (1.0 / 8192.0)
             ssq[...] = jnp.broadcast_to(lax.rsqrt(mean + EPSILON), ssq.shape)
+            local[6].wait()
         if t == 2:
-            local[6].wait()
             lax.fori_loop(0, 16, scale_group, 0)
+            for i in (0, 1, 2, 3, 8, 9, 10, 11):
+                norm_copy(i).start()
         if t == 3:
             lax.fori_loop(16, 32, scale_group, 0)
-            for copy in norm_copies:
-                copy.start()
+            for i in (4, 5, 6, 7, 12, 13, 14, 15):
+                norm_copy(i).start()
+            local[1].wait()
         if t == 4:
-            local[1].wait()
-            lax.fori_loop(0, 32, lora_group, 0)
+            lax.fori_loop(0, 16, lora_group, 0)
+        if t == 5:
+            lax.fori_loop(16, 32, lora_group, 0)
             local[0].wait()
             local[7].wait()
-            acc[...] = jnp.broadcast_to(bias_ref[...].astype(jnp.float32).reshape(1, 768), acc.shape)
+            acc[mine, :] = jnp.broadcast_to(bias_ref[...].astype(jnp.float32).reshape(1, 768), (256, 768))
+            acc[others, :] = jnp.zeros((256, 768), jnp.float32)
+            for i in range(16):
+                norm_copy(i).wait_recv()
         if t == 6:
             for i in (3, 4, 5, 8):
                 local[i].wait()
@@ -266,31 +270,23 @@
                 flags[me_d, pl.ds(r, 1), :] = jnp.full((1, 128), assign_ref[r], jnp.int32)
             for copy in flag_copies:
                 copy.start()
-        if t >= 5:
-            for s in [s for s in mates if s < t]:
-                for key in mates.pop(s):
-                    core_landing(*key).wait_recv()
-                    ready.append(key + (0,))
-            if ready:
-                multiply(ready)
-                ready = []
-    last = [key for s in mates for key in mates[s]]
-    for key in last:
-        core_landing(*key).wait_recv()
-    if last:
-        multiply([key + (0,) for key in last])
+        if 6 <= t < n_steps - 1 and ready:
+            multiply(ready, slice(0, 512))
+            ready = []
+    multiply(ready, others)
+    part_copy(0).start()
+    part_copy(1).start()
+    multiply(ready, mine)
 
     low = low2[...].astype(jnp.bfloat16)
     low_wide = jnp.concatenate([low, low], axis=1)
     lora = jnp.dot(low, up_ref[...], preferred_element_type=jnp.float32)
-    qbuf[...] = (acc[:, :512] + ADAPTER_SCALE * lora).astype(jnp.bfloat16)
-    kbuf[...] = acc[:, 512:640].astype(jnp.bfloat16)
-    vbuf[...] = acc[:, 640:].astype(jnp.bfloat16)
     row = lax.broadcasted_iota(jnp.int32, (128, 128), 0)
     col = lax.broadcasted_iota(jnp.int32, (128, 128), 1)
     same = (row // 32) == (col // 32)
     causal = same & ((col % 32) <= (row % 32))
     scale = 128 ** (-0.5)
+    heads = [slice(h * 128, h * 128 + 128) for h in range(4)]
 
     def spread(ref, half, where, kind):
         out = jnp.full((128, 128), ref[half * 4].astype(kind), kind)
@@ -298,22 +294,26 @@
             out = jnp.where(where // 32 == r, jnp.full((128, 128), ref[half * 4 + r].astype(kind), kind), out)
         return out
 
-    lives = []
+    lives = [(row % 32) < spread(len_ref, half, row, jnp.int32) for half in range(2)]
+    seen = [causal & ((col % 32) < spread(len_ref, half, col, jnp.int32)) for half in range(2)]
     for half in range(2):
         rows = slice(half * 128, half * 128 + 128)
-        visible = causal & ((col % 32) < spread(len_ref, half, col, jnp.int32))
-        live = (row % 32) < spread(len_ref, half, row, jnp.int32)
-        lives.append(live)
-        for h in range(4):
-            cols = slice(h * 128, h * 128 + 128)
-            scores = lax.dot_general(qbuf[rows, cols], kbuf[rows, :], NT, preferred_element_type=jnp.float32)
-            scores = jnp.where(visible, scores * scale, jnp.float32(-1e30))
-            raised = jnp.exp(scores - jnp.max(scores, axis=-1, keepdims=True))
-            soft = raised / jnp.sum(raised, axis=-1, keepdims=True)
-            pbuf[half * 4 + h] = soft
-            out = jnp.dot(soft.astype(jnp.bfloat16), vbuf[rows, :], preferred_element_type=jnp.float32)
-            out = jnp.where(live, out, 0.0).astype(jnp.bfloat16)
-            attb[half * 4 : half * 4 + 4, :, cols] = out.reshape(4, 32, 128)
+        part_copy(half).wait_recv()
+        projected = acc[rows, :] + part_acc[rows, :]
+        queries = (projected[:, :512] + ADAPTER_SCALE * lora[rows, :]).astype(jnp.bfloat16)
+        keys = projected[:, 512:640].astype(jnp.bfloat16)
+        values = projected[:, 640:].astype(jnp.bfloat16)
+        kbuf[rows, :] = keys
+        vbuf[rows, :] = values
+        scores = [lax.dot_general(queries[:, h], keys, NT, preferred_element_type=jnp.float32) for h in heads]
+        scores = [jnp.where(seen[half], s * scale, jnp.float32(-1e30)) for s in scores]
+        raised = [jnp.exp(s - jnp.max(s, axis=-1, keepdims=True)) for s in scores]
+        soft = [r / jnp.sum(r, axis=-1, keepdims=True) for r in raised]
+        outs = [jnp.dot(p.astype(jnp.bfloat16), values, preferred_element_type=jnp.float32) for p in soft]
+        for i, h in enumerate(heads):
+            pbuf[half * 4 + i] = soft[i]
+            out = jnp.where(lives[half], outs[i], 0.0).astype(jnp.bfloat16)
+            attb[half * 4 : half * 4 + 4, :, h] = out.reshape(4, 32, 128)
 
     def fill_slot(d, carry):
         which = jnp.int32(0)
@@ -338,21 +338,21 @@
     for half in range(2):
         rows = slice(half * 128, half * 128 + 128)
         factor = spread(adv_ref, half, row, jnp.float32) / spread(len_ref, half, row, jnp.float32)
-        for h in range(4):
-            cols = slice(h * 128, h * 128 + 128)
-            weighted = (og_ref[rows, cols].astype(jnp.float32) * factor).astype(jnp.bfloat16)
-            weighted = jnp.where(lives[half], weighted.astype(jnp.float32), 0.0).astype(jnp.bfloat16)
-            dsoft = lax.dot_general(weighted, vbuf[rows, :], NT, preferred_element_type=jnp.float32)
-            dsoft = dsoft.astype(jnp.bfloat16).astype(jnp.float32)
-            soft = pbuf[half * 4 + h]
-            inner = jnp.sum(dsoft * soft, axis=-1, keepdims=True)
-            dscores = (soft * (dsoft - inner) * scale).astype(jnp.bfloat16)
-            dquery = jnp.dot(dscores, kbuf[rows, :], preferred_element_type=jnp.float32)
-            qg[rows, cols] = dquery.astype(jnp.bfloat16)
+        keys, values = kbuf[rows, :], vbuf[rows, :]
+        weighted = [(og_ref[rows, h].astype(jnp.float32) * factor).astype(jnp.bfloat16) for h in heads]
+        weighted = [jnp.where(lives[half], w.astype(jnp.float32), 0.0).astype(jnp.bfloat16) for w in weighted]
+        dsoft = [lax.dot_general(w, values, NT, preferred_element_type=jnp.float32) for w in weighted]
+        dsoft = [d.astype(jnp.bfloat16).astype(jnp.float32) for d in dsoft]
+        soft = [pbuf[half * 4 + i] for i in range(4)]
+        inner = [jnp.sum(d * p, axis=-1, keepdims=True) for d, p in zip(dsoft, soft)]
+        dscores = [(p * (d - i) * scale).astype(jnp.bfloat16) for d, p, i in zip(dsoft, soft, inner)]
+        dquery = [jnp.dot(d, keys, preferred_element_type=jnp.float32) for d in dscores]
+        for d, h in zip(dquery, heads):
+            qg[rows, h] = d.astype(jnp.bfloat16)
     low_grad = ADAPTER_SCALE * lax.dot_general(up_ref[...], qg[...], NT, preferred_element_type=jnp.float32)
-    lg[0] = low_grad.astype(jnp.bfloat16)
+    lg[:, :256] = low_grad.astype(jnp.bfloat16)
     lg_copy = pltpu.make_async_remote_copy(
-        src_ref=lg.at[0], dst_ref=lg.at[1], send_sem=msem.at[0, 16], recv_sem=msem.at[1, 16],
+        src_ref=lg.at[:, pl.ds(0, 256)], dst_ref=lg.at[:, pl.ds(256, 256)], send_sem=msem.at[0, 16], recv_sem=msem.at[1, 16],
         device_id=mate, device_id_type=MESH,
     )
     lg_copy.start()
@@ -360,15 +360,11 @@
     up_four = up_grad.reshape(16, 2, 16, 128)
     lane = lax.broadcasted_iota(jnp.int32, (16, 16, 128), 2)
     ordered[...] = jnp.where(lane < 64, up_four[:, 0], up_four[:, 1]).astype(jnp.bfloat16)
-    for copy in norm_copies:
-        copy.wait()
     lg_copy.wait()
 
     def down_slice(i, carry):
         d = (me_d + lookup(i, ORDER)) % 16
-        part = jnp.dot(lg[0], nbuf[2 * d + c], preferred_element_type=jnp.float32)
-        part += jnp.dot(lg[1], mnorm[d], preferred_element_type=jnp.float32)
-        part = part.astype(jnp.bfloat16)
+        part = jnp.dot(lg[...], nbuf[2 * d + c], preferred_element_type=jnp.float32).astype(jnp.bfloat16)
         for i2 in range(4):
             for j2 in range(2):
                 pay_a[j2 * 4 + i2, i] = part[i2 * 16 : i2 * 16 + 16, j2 * 128 : j2 * 128 + 128]
@@ -388,8 +384,10 @@
             a_copy(q, k).start()
     for e in range(N_ENTRIES):
         piece_send(e).wait_send()
-    for key in [(0, 0, 0), (0, 0, 1)] + list(GROUP_DONE):
-        core_send(*key).wait_send()
+    for i in range(16):
+        norm_copy(i).wait_send()
+    for half in range(2):
+        part_copy(half).wait_send()
     for copy in flag_copies:
         copy.wait()
     b_copies = [
@@ -487,19 +485,18 @@
             pltpu.VMEM((64, 512), bf16),
             pltpu.VMEM((256, 512), bf16),
             pltpu.VMEM((32, 256, 256), bf16),
-            pltpu.VMEM((32, 256, 256), bf16),
-            pltpu.VMEM((16, 256, 256), bf16),
-            pltpu.VMEM((16, 512, 768), bf16),
+            pltpu.VMEM((32, 512, 256), bf16),
+            pltpu.VMEM((8, 512, 768), bf16),
+            pltpu.VMEM((512, 768), f32),
             pltpu.VMEM((256, 768), f32),
             pltpu.VMEM((256, 128), f32),
-            pltpu.VMEM((256, 512), bf16),
             pltpu.VMEM((256, 128), bf16),
             pltpu.VMEM((256, 128), bf16),
             pltpu.VMEM((256, 64), f32),
             pltpu.VMEM((8, 32, 512), bf16),
             pltpu.VMEM((8, 128, 128), f32),
             pltpu.VMEM((256, 512), bf16),
-            pltpu.VMEM((2, 64, 256), bf16),
+            pltpu.VMEM((64, 512), bf16),
             pltpu.VMEM((16, 8, 128), jnp.int32),
             pltpu.VMEM((16, 32, 512), bf16),
             pltpu.VMEM((16, 32, 512), bf16),
@@ -510,8 +507,8 @@
             pltpu.VMEM((15, 2, 16, 128), bf16),
             pltpu.VMEM((2, 16, 128), bf16),
             pltpu.SemaphoreType.REGULAR((5,)),
-            dma((32,)), dma((11,)), dma((N_ENTRIES,)), dma((N_ENTRIES,)), dma((16,)), dma((16,)),
-            dma((2, 17)), dma((15,)), dma((15,)), dma((15,)), dma((15,)), dma((16 // CHUNK, 7)), dma((16 // CHUNK, 7)),
+            dma((32,)), dma((11,)), dma((N_ENTRIES,)), dma((N_ENTRIES,)),
+            dma((2, 19)), dma((15,)), dma((15,)), dma((15,)), dma((15,)), dma((16 // CHUNK, 7)), dma((16 // CHUNK, 7)),
             dma((15,)), dma((15,)), dma((15,)), dma((15,)),
         ],
         compiler_params=pltpu.CompilerParams(

time: 77.2 us -> 68.5 us (0.89)
  Pallas kernels: 76.5 us -> 67.8 us
    pallas_call x1, Pallas kernels: 74.7 us -> 66 us  [on_device(): pl.pallas_call(kernel, out_shape=(jax.ShapeDtypeStruct((8, 32, 512), bf16...]
where the time goes in v4:
time: 68.5 us; the launch traced here: 68.4 us
  Pallas kernels  67.8 us (99%)
    pallas_call x1, Pallas kernels, on_device(): pl.pallas_call(kernel, out_shape=(jax.ShapeDtypeStruct((8, 32, 512), bf16...  66 us
    pallas_call x1, Pallas kernels, on_device(): pl.pallas_call(assemble, out_shape=(jax.ShapeDtypeStruct((8, 32, 512), bf...  1.75 us

profile of v4, /device:TPU:1, one launch (start us, length us, event | category | flops | bytes accessed | tf_op | source)
XLA Modules:
  0.0 68.4 jit_solution(7251064231466183045)
XLA Ops:
  0.6 66.0 %block.1 = (bf16[8,32,512]{2,1,0:T(8,128)(2,1)}, bf16[16,2,16,128]{3,2,1,0:T(8,128)(2,1)}) custom-call(s32[8]{0:T(128)} %len_hbm.1, s32[8]{0:T(128)} %assign_hbm.1, f32[8]{0:T(128)} %adv_hbm.1, bf16[256,8192]{1,0:T(8,128)(2,1)} %bitcast.6, f32[1,8192]{1,0:T(1,128)} %bitcast.9, bf16[512,768]{1,0:T(8,128)(2,1)} %w_ref.1, bf16[768]{0:T(1024)(128)(2,1)} %bias_hbm.1, ...), custom_call_target="tpu_custom_call" | custom-call | tf_op jit(solution)/shard_map/block/pallas_call | solution.py:473
  66.7 1.8 %assemble.1 = (bf16[8,32,512]{2,1,0:T(8,128)(2,1)}, f32[64,512]{1,0:T(8,128)}, f32[32,64]{1,0:T(8,128)}) custom-call(bf16[8,32,512]{2,1,0:T(8,128)(2,1)} %get-tuple-element.8.att_ref, bf16[16,2,16,128]{3,2,1,0:T(8,128)(2,1)} %get-tuple-element.9.sums_ref), custom_call_target="tpu_custom_call" | custom-call | tf_op jit(solution)/shard_map/assemble/pallas_call | solution.py:530

commit v5 on v4

--- a/solution.py
+++ b/solution.py
@@ -28,7 +28,8 @@
 N_ENTRIES = len(ENTRIES)
 GAP = 3
 PIECE = 64
-ORDER = (7, 8, 9, 10, 6, 5, 11, 12, 4, 3, 13, 14, 2, 1, 15, 0)
+ORDER = (7, 8, 9, 10, 6, 5, 11, 12, 4, 3, 13, 14, 2, 1, 15)
+Z_ORDER = (4, 3, 5, 2, 6, 1, 7, 0)
 CHUNK = 4
 GROUP = 256
 
@@ -53,6 +54,9 @@
 
 GROUP_DONE = group_plan()
 AHEAD = 1
+LATE_FROM = len(SCHEDULE) - 1
+LATE = tuple(key for key in GROUP_DONE if GROUP_DONE[key] >= LATE_FROM)
+SPLIT = 6
 
 
 def issue_plan():
@@ -81,9 +85,9 @@
     len_hbm, assign_hbm, adv_hbm, hid_ref, gain_hbm, w_ref, bias_hbm, ad_hbm, up_hbm, og_hbm,
     att_out, rec_c,
     len_ref, assign_ref, adv_ref, gain_ref, bias_ref, ad_ref, up_ref, og_ref,
-    hbuf, nbuf, wbuf, acc, part_acc, ssq, kbuf, vbuf, low2, attb, pbuf, qg, lg,
+    hbuf, nbuf, wbuf, wlate, acc, part_acc, ssq, kbuf, vbuf, low2, attb, pbuf, qg, lg,
     flags, pay_s, rec_s, ordered, pay_a, rec_a, pay_b, rec_b, pay_c,
-    tokens, hsem, lsem, wsend, wrecv, msem, fsem, frecv, ssem, srecv, asem, arecv, bsem,
+    tokens, hsem, lsem, wsend, wrecv, psend, precv, msem, fsem, frecv, ssem, srecv, asem, arecv, bsem,
     brecv, gsem, grecv,
 ):
     me_d, me_f = lax.axis_index("dp"), lax.axis_index("fsdp")
@@ -102,6 +106,7 @@
         at(z, y, x + 3), at(z, y, x + 1), at(z, y + 3, x), at(z, y + 1, x), at(z + 7, y, x), at(z + 1, y, x),
     )
     neighbours = receivers + (mate,)
+    y_pair, y_cross = y + 1 - 2 * yl, y - 1 + 2 * yl + 4
     f_peers = [(me_d, (me_f + k) % 16) for k in range(1, 16)]
     d_peers = [((me_d + k) % 16, me_f) for k in range(1, 16)]
 
@@ -167,6 +172,21 @@
             device_id=mate, device_id_type=MESH,
         )
 
+    def pass_on(i, v):
+        dx, dy, h = LATE[i]
+        k = v + par if v % 2 == 0 else v - par
+        return pltpu.make_async_remote_copy(
+            src_ref=wbuf.at[shard(dx, dy), rows_of(v)],
+            dst_ref=wlate.at[i, pl.ds(pl.multiple_of((k - 4 * h) * PIECE, PIECE), PIECE)],
+            send_sem=psend.at[4 * i + v - 4 * h], recv_sem=precv.at[4 * i + v - 4 * h],
+            device_id=mate, device_id_type=MESH,
+        )
+
+    def multiply_late(i):
+        dx, dy, h = LATE[i]
+        g = (2 * shard(dx, dy) + 1 - c) * 2 + h
+        acc[:256, :] += jnp.dot(nbuf[g, :256, :], wlate[i], preferred_element_type=jnp.float32)
+
     def multiply(items, rows):
         def body(i, carry):
             j = shard(lookup(i, [item[0] for item in items]), lookup(i, [item[1] for item in items]))
@@ -228,6 +248,9 @@
         if t >= GAP:
             for e in by_step[t - GAP]:
                 piece_landing(e).wait_recv()
+                _, _, dx, dy, v = ENTRIES[e]
+                if (dx, dy, v // 4) in LATE:
+                    pass_on(LATE.index((dx, dy, v // 4)), v).start()
         for e in ISSUE[t]:
             piece_send(e).start()
         if 1 <= t <= 5:
@@ -235,7 +258,7 @@
         if t < 5:
             send_tokens(t)
         for key, done in GROUP_DONE.items():
-            if done == t - GAP:
+            if done == t - GAP and key not in LATE:
                 ready.append(key)
         if t == 0:
             lax.fori_loop(0, 16, sum_squares, 0)
@@ -270,13 +293,17 @@
                 flags[me_d, pl.ds(r, 1), :] = jnp.full((1, 128), assign_ref[r], jnp.int32)
             for copy in flag_copies:
                 copy.start()
-        if 6 <= t < n_steps - 1 and ready:
+        if t >= 6 and ready:
             multiply(ready, slice(0, 512))
             ready = []
-    multiply(ready, others)
-    part_copy(0).start()
-    part_copy(1).start()
-    multiply(ready, mine)
+        if t == LATE_FROM - 1 + GAP:
+            part_copy(0).start()
+            part_copy(1).start()
+    multiply(LATE, mine)
+    for i in range(len(LATE)):
+        for v in range(4 * LATE[i][2], 4 * LATE[i][2] + 4):
+            pass_on(i, v).wait_recv()
+        multiply_late(i)
 
     low = low2[...].astype(jnp.bfloat16)
     low_wide = jnp.concatenate([low, low], axis=1)
@@ -326,12 +353,12 @@
     rec_s[me_d] = pay_s[me_d]
     slot_copies = [
         pltpu.make_async_remote_copy(
-            src_ref=pay_s.at[d_peers[k][0]], dst_ref=rec_s.at[me_d], send_sem=ssem.at[k], recv_sem=srecv.at[k],
-            device_id=d_peers[k], device_id_type=MESH,
-        )
-        for k in range(15)
+            src_ref=pay_s.at[(me_d + ORDER[i]) % 16], dst_ref=rec_s.at[me_d], send_sem=ssem.at[i],
+            recv_sem=srecv.at[i], device_id=((me_d + ORDER[i]) % 16, me_f), device_id_type=MESH,
+        )
+        for i in range(15)
     ]
-    for copy in slot_copies:
+    for copy in slot_copies[:SPLIT]:
         copy.start()
 
     local[2].wait()
@@ -363,7 +390,7 @@
     lg_copy.wait()
 
     def down_slice(i, carry):
-        d = (me_d + lookup(i, ORDER)) % 16
+        d = (z + lookup(i // 2, Z_ORDER)) % 8 * 2 + i % 2
         part = jnp.dot(lg[...], nbuf[2 * d + c], preferred_element_type=jnp.float32).astype(jnp.bfloat16)
         for i2 in range(4):
             for j2 in range(2):
@@ -372,9 +399,12 @@
 
     def a_copy(q, k):
         span = pl.ds(q * CHUNK, CHUNK)
-        return pltpu.make_async_remote_copy(
-            src_ref=pay_a.at[(chip + k) % 8, span], dst_ref=rec_a.at[k - 1, span], send_sem=asem.at[q, k - 1],
-            recv_sem=arecv.at[q, k - 1], device_id=(me_d, ((chip + k) % 8) * 2 + c), device_id_type=MESH,
+        there = (chip + k) % 8
+        other = (there // 4 + yl) % 2
+        y_to = y + other * ((y_cross if q % 2 else y_pair) - y)
+        return pltpu.make_async_remote_copy(
+            src_ref=pay_a.at[there, span], dst_ref=rec_a.at[k - 1, span], send_sem=asem.at[q, k - 1],
+            recv_sem=arecv.at[q, k - 1], device_id=at(z, y_to, there % 4), device_id_type=MESH,
         )
 
     chunks = range(16 // CHUNK)
@@ -388,15 +418,27 @@
         norm_copy(i).wait_send()
     for half in range(2):
         part_copy(half).wait_send()
+    for i in range(len(LATE)):
+        for v in range(4 * LATE[i][2], 4 * LATE[i][2] + 4):
+            pass_on(i, v).wait_send()
     for copy in flag_copies:
         copy.wait()
-    b_copies = [
-        pltpu.make_async_remote_copy(
-            src_ref=pay_b.at[i], dst_ref=rec_b.at[i], send_sem=bsem.at[i], recv_sem=brecv.at[i],
-            device_id=((me_d + ORDER[i]) % 16, me_f), device_id_type=MESH,
-        )
-        for i in range(15)
-    ]
+    def slice_at(i):
+        return (z + Z_ORDER[i // 2]) % 8 * 2 + i % 2
+
+    def b_copy(i):
+        slot = i - i % 2 + yh if i < 14 else 14
+        return pltpu.make_async_remote_copy(
+            src_ref=pay_b.at[i if i < 14 else 15 - yh], dst_ref=rec_b.at[slot], send_sem=bsem.at[i],
+            recv_sem=brecv.at[slot], device_id=(slice_at(i) if i < 14 else 2 * z + 1 - yh, me_f), device_id_type=MESH,
+        )
+
+    def b_landing(slot):
+        return pltpu.make_async_remote_copy(
+            src_ref=rec_b.at[slot], dst_ref=rec_b.at[slot], send_sem=bsem.at[slot], recv_sem=brecv.at[slot],
+            device_id=mate, device_id_type=MESH,
+        )
+
     for q in chunks:
         span = pl.ds(q * CHUNK, CHUNK)
         for k in range(1, 8):
@@ -406,10 +448,31 @@
             total += rec_a[k, span].astype(jnp.float32)
         pay_b[span, 0] = total.astype(jnp.bfloat16)
         for i in range(q * CHUNK, (q + 1) * CHUNK):
-            pay_b[i, 1] = ordered[(me_d + ORDER[i]) % 16]
-            if i < 15:
-                b_copies[i].start()
-
+            pay_b[i, 1] = ordered[slice_at(i)]
+            if i < 14:
+                b_copy(i).start()
+    b_copy(14).start()
+
+    for copy in slot_copies[SPLIT:]:
+        copy.start()
+    for i in range(15):
+        b_copy(i).wait_send()
+        b_landing(i).wait_recv()
+    total = pay_b[14 + yh].astype(jnp.float32)
+    for k in range(15):
+        total += rec_b[k].astype(jnp.float32)
+    pay_c[...] = total.astype(jnp.bfloat16)
+    c_copies = [
+        pltpu.make_async_remote_copy(
+            src_ref=pay_c, dst_ref=rec_c.at[me_f], send_sem=gsem.at[k], recv_sem=grecv.at[k],
+            device_id=f_peers[k], device_id_type=MESH,
+        )
+        for k in range(15)
+    ]
+    for copy in c_copies:
+        copy.start()
+    own_copy = pltpu.make_async_copy(pay_c, rec_c.at[me_f], lsem.at[10])
+    own_copy.start()
     for copy in slot_copies:
         copy.wait()
     held = [jnp.sum((flags[s] == me_d).astype(jnp.float32), axis=0, keepdims=True) for s in range(16)]
@@ -425,23 +488,6 @@
     att_copy = pltpu.make_async_copy(attb, att_out, lsem.at[9])
     att_copy.start()
 
-    for copy in b_copies:
-        copy.wait()
-    total = pay_b[15].astype(jnp.float32)
-    for k in range(15):
-        total += rec_b[k].astype(jnp.float32)
-    pay_c[...] = total.astype(jnp.bfloat16)
-    c_copies = [
-        pltpu.make_async_remote_copy(
-            src_ref=pay_c, dst_ref=rec_c.at[me_f], send_sem=gsem.at[k], recv_sem=grecv.at[k],
-            device_id=f_peers[k], device_id_type=MESH,
-        )
-        for k in range(15)
-    ]
-    for copy in c_copies:
-        copy.start()
-    own_copy = pltpu.make_async_copy(pay_c, rec_c.at[me_f], lsem.at[10])
-    own_copy.start()
     for copy in c_copies:
         copy.wait()
     own_copy.wait()
@@ -487,6 +533,7 @@
             pltpu.VMEM((32, 256, 256), bf16),
             pltpu.VMEM((32, 512, 256), bf16),
             pltpu.VMEM((8, 512, 768), bf16),
+            pltpu.VMEM((len(LATE), 256, 768), bf16),
             pltpu.VMEM((512, 768), f32),
             pltpu.VMEM((256, 768), f32),
             pltpu.VMEM((256, 128), f32),
@@ -507,7 +554,7 @@
             pltpu.VMEM((15, 2, 16, 128), bf16),
             pltpu.VMEM((2, 16, 128), bf16),
             pltpu.SemaphoreType.REGULAR((5,)),
-            dma((32,)), dma((11,)), dma((N_ENTRIES,)), dma((N_ENTRIES,)),
+            dma((32,)), dma((11,)), dma((N_ENTRIES,)), dma((N_ENTRIES,)), dma((4 * len(LATE),)), dma((4 * len(LATE),)),
             dma((2, 19)), dma((15,)), dma((15,)), dma((15,)), dma((15,)), dma((16 // CHUNK, 7)), dma((16 // CHUNK, 7)),
             dma((15,)), dma((15,)), dma((15,)), dma((15,)),
         ],

time: 68.5 us -> 65.4 us (0.955)
  Pallas kernels: 67.8 us -> 64.6 us
    pallas_call x1, Pallas kernels: 66 us -> 62.9 us  [on_device(): pl.pallas_call(kernel, out_shape=(jax.ShapeDtypeStruct((8, 32, 512), bf16...]
where the time goes in v5:
time: 65.4 us; the launch traced here: 65.3 us
  Pallas kernels  64.6 us (99%)
    pallas_call x1, Pallas kernels, on_device(): pl.pallas_call(kernel, out_shape=(jax.ShapeDtypeStruct((8, 32, 512), bf16...  62.9 us
    pallas_call x1, Pallas kernels, on_device(): pl.pallas_call(assemble, out_shape=(jax.ShapeDtypeStruct((8, 32, 512), bf...  1.75 us

profile of v5, /device:TPU:1, one launch (start us, length us, event | category | flops | bytes accessed | tf_op | source)
XLA Modules:
  0.0 65.3 jit_solution(12804777631316471991)
XLA Ops:
  0.6 62.9 %block.1 = (bf16[8,32,512]{2,1,0:T(8,128)(2,1)}, bf16[16,2,16,128]{3,2,1,0:T(8,128)(2,1)}) custom-call(s32[8]{0:T(128)} %len_hbm.1, s32[8]{0:T(128)} %assign_hbm.1, f32[8]{0:T(128)} %adv_hbm.1, bf16[256,8192]{1,0:T(8,128)(2,1)} %bitcast.6, f32[1,8192]{1,0:T(1,128)} %bitcast.9, bf16[512,768]{1,0:T(8,128)(2,1)} %w_ref.1, bf16[768]{0:T(1024)(128)(2,1)} %bias_hbm.1, ...), custom_call_target="tpu_custom_call" | custom-call | tf_op jit(solution)/shard_map/block/pallas_call | solution.py:519
  63.5 1.8 %assemble.1 = (bf16[8,32,512]{2,1,0:T(8,128)(2,1)}, f32[64,512]{1,0:T(8,128)}, f32[32,64]{1,0:T(8,128)}) custom-call(bf16[8,32,512]{2,1,0:T(8,128)(2,1)} %get-tuple-element.8.att_ref, bf16[16,2,16,128]{3,2,1,0:T(8,128)(2,1)} %get-tuple-element.9.sums_ref), custom_call_target="tpu_custom_call" | custom-call | tf_op jit(solution)/shard_map/assemble/pallas_call | solution.py:577

commit v6 on v5

--- a/solution.py
+++ b/solution.py
@@ -107,23 +107,13 @@
     )
     neighbours = receivers + (mate,)
     y_pair, y_cross = y + 1 - 2 * yl, y - 1 + 2 * yl + 4
-    f_peers = [(me_d, (me_f + k) % 16) for k in range(1, 16)]
+    f_peers = [(me_d, (me_f + k) % 16) for k in (4, 12, 5, 3, 11, 13, 2, 14, 6, 10, 7, 9, 8, 15, 1)]
     d_peers = [((me_d + k) % 16, me_f) for k in range(1, 16)]
 
     barrier = pltpu.get_barrier_semaphore()
     for peer in neighbours:
         pl.semaphore_signal(barrier, inc=1, device_id=peer, device_id_type=MESH)
 
-    def hidden_copy(g):
-        return pltpu.make_async_copy(
-            hid_ref.at[:, pl.ds(pl.multiple_of(g * GROUP, GROUP), GROUP)], hbuf.at[g], hsem.at[g]
-        )
-
-    def start_hidden(g, carry):
-        hidden_copy(g).start()
-        return carry
-
-    lax.fori_loop(0, 32, start_hidden, 0)
     local = [
         pltpu.make_async_copy(src, dst, lsem.at[i])
         for i, (src, dst) in enumerate((
@@ -131,12 +121,16 @@
             (adv_hbm, adv_ref), (gain_hbm, gain_ref), (bias_hbm, bias_ref), (up_hbm, up_ref),
         ))
     ]
-    for copy in local:
-        copy.start()
-    ssq[...] = jnp.zeros_like(ssq)
-    low2[...] = jnp.zeros_like(low2)
-
     pl.semaphore_wait(barrier, 7)
+
+    def hidden_copy(g):
+        return pltpu.make_async_copy(
+            hid_ref.at[:, pl.ds(pl.multiple_of(g * GROUP, GROUP), GROUP)], hbuf.at[g], hsem.at[g]
+        )
+
+    def start_hidden(g, carry):
+        hidden_copy(g).start()
+        return carry
 
     def send_tokens(i):
         for peer in neighbours:
@@ -261,6 +255,11 @@
             if done == t - GAP and key not in LATE:
                 ready.append(key)
         if t == 0:
+            lax.fori_loop(0, 32, start_hidden, 0)
+            for copy in local:
+                copy.start()
+            ssq[...] = jnp.zeros_like(ssq)
+            low2[...] = jnp.zeros_like(low2)
             lax.fori_loop(0, 16, sum_squares, 0)
         if t == 1:
             lax.fori_loop(16, 32, sum_squares, 0)
@@ -430,13 +429,7 @@
         slot = i - i % 2 + yh if i < 14 else 14
         return pltpu.make_async_remote_copy(
             src_ref=pay_b.at[i if i < 14 else 15 - yh], dst_ref=rec_b.at[slot], send_sem=bsem.at[i],
-            recv_sem=brecv.at[slot], device_id=(slice_at(i) if i < 14 else 2 * z + 1 - yh, me_f), device_id_type=MESH,
-        )
-
-    def b_landing(slot):
-        return pltpu.make_async_remote_copy(
-            src_ref=rec_b.at[slot], dst_ref=rec_b.at[slot], send_sem=bsem.at[slot], recv_sem=brecv.at[slot],
-            device_id=mate, device_id_type=MESH,
+            recv_sem=brecv.at[0], device_id=(slice_at(i) if i < 14 else 2 * z + 1 - yh, me_f), device_id_type=MESH,
         )
 
     for q in chunks:
@@ -455,16 +448,14 @@
 
     for copy in slot_copies[SPLIT:]:
         copy.start()
-    for i in range(15):
-        b_copy(i).wait_send()
-        b_landing(i).wait_recv()
+    pltpu.make_async_copy(rec_b, rec_b, brecv.at[0]).wait()
     total = pay_b[14 + yh].astype(jnp.float32)
     for k in range(15):
         total += rec_b[k].astype(jnp.float32)
     pay_c[...] = total.astype(jnp.bfloat16)
     c_copies = [
         pltpu.make_async_remote_copy(
-            src_ref=pay_c, dst_ref=rec_c.at[me_f], send_sem=gsem.at[k], recv_sem=grecv.at[k],
+            src_ref=pay_c, dst_ref=rec_c.at[me_f], send_sem=gsem.at[0], recv_sem=grecv.at[0],
             device_id=f_peers[k], device_id_type=MESH,
         )
         for k in range(15)
@@ -488,8 +479,11 @@
     att_copy = pltpu.make_async_copy(attb, att_out, lsem.at[9])
     att_copy.start()
 
-    for copy in c_copies:
-        copy.wait()
+    for i in range(15):
+        b_copy(i).wait_send()
+    most = rec_c.at[pl.ds(0, 15)]
+    pltpu.make_async_copy(most, most, grecv.at[0]).wait()
+    pltpu.make_async_copy(most, most, gsem.at[0]).wait()
     own_copy.wait()
     att_copy.wait()
 
@@ -556,7 +550,7 @@
             pltpu.SemaphoreType.REGULAR((5,)),
             dma((32,)), dma((11,)), dma((N_ENTRIES,)), dma((N_ENTRIES,)), dma((4 * len(LATE),)), dma((4 * len(LATE),)),
             dma((2, 19)), dma((15,)), dma((15,)), dma((15,)), dma((15,)), dma((16 // CHUNK, 7)), dma((16 // CHUNK, 7)),
-            dma((15,)), dma((15,)), dma((15,)), dma((15,)),
+            dma((15,)), dma((1,)), dma((1,)), dma((1,)),
         ],
         compiler_params=pltpu.CompilerParams(
             collective_id=0, has_side_effects=True, vmem_limit_bytes=56 * 2**20

time: 65.4 us -> 64.8 us (level)
  no operation moved by 1% of the time
where the time goes in v6:
time: 64.8 us; the launch traced here: 64.7 us
  Pallas kernels  64 us (99%)
    pallas_call x1, Pallas kernels, on_device(): pl.pallas_call(kernel, out_shape=(jax.ShapeDtypeStruct((8, 32, 512), bf16...  62.3 us
    pallas_call x1, Pallas kernels, on_device(): pl.pallas_call(assemble, out_shape=(jax.ShapeDtypeStruct((8, 32, 512), bf...  1.75 us

profile of v6, /device:TPU:1, one launch (start us, length us, event | category | flops | bytes accessed | tf_op | source)
XLA Modules:
  0.0 64.7 jit_solution(9964592051755972384)
XLA Ops:
  0.6 62.3 %block.1 = (bf16[8,32,512]{2,1,0:T(8,128)(2,1)}, bf16[16,2,16,128]{3,2,1,0:T(8,128)(2,1)}) custom-call(s32[8]{0:T(128)} %len_hbm.1, s32[8]{0:T(128)} %assign_hbm.1, f32[8]{0:T(128)} %adv_hbm.1, bf16[256,8192]{1,0:T(8,128)(2,1)} %bitcast.6, f32[1,8192]{1,0:T(1,128)} %bitcast.9, bf16[512,768]{1,0:T(8,128)(2,1)} %w_ref.1, bf16[768]{0:T(1024)(128)(2,1)} %bias_hbm.1, ...), custom_call_target="tpu_custom_call" | custom-call | tf_op jit(solution)/shard_map/block/pallas_call | solution.py:513
  62.9 1.8 %assemble.1 = (bf16[8,32,512]{2,1,0:T(8,128)(2,1)}, f32[64,512]{1,0:T(8,128)}, f32[32,64]{1,0:T(8,128)}) custom-call(bf16[8,32,512]{2,1,0:T(8,128)(2,1)} %get-tuple-element.8.att_ref, bf16[16,2,16,128]{3,2,1,0:T(8,128)(2,1)} %get-tuple-element.9.sums_ref), custom_call_target="tpu_custom_call" | custom-call | tf_op jit(solution)/shard_map/assemble/pallas_call | solution.py:571

commit v7 on v6

--- a/solution.py
+++ b/solution.py
@@ -233,6 +233,19 @@
             src_ref=acc.at[pl.ds(256 + half * 128, 128)], dst_ref=part_acc.at[rows],
             send_sem=msem.at[0, 17 + half], recv_sem=msem.at[1, 17 + half], device_id=mate, device_id_type=MESH,
         )
+
+    row = lax.broadcasted_iota(jnp.int32, (128, 128), 0)
+    col = lax.broadcasted_iota(jnp.int32, (128, 128), 1)
+    same = (row // 32) == (col // 32)
+    causal = same & ((col % 32) <= (row % 32))
+    scale = 128 ** (-0.5)
+    heads = [slice(h * 128, h * 128 + 128) for h in range(4)]
+
+    def spread(ref, half, where, kind):
+        out = jnp.full((128, 128), ref[half * 4].astype(kind), kind)
+        for r in range(1, 4):
+            out = jnp.where(where // 32 == r, jnp.full((128, 128), ref[half * 4 + r].astype(kind), kind), out)
+        return out
 
     by_step = [[e for e in range(N_ENTRIES) if ENTRIES[e][0] == t] for t in range(len(SCHEDULE))]
     ready = [(0, 0, 0), (0, 0, 1)]
@@ -286,8 +299,17 @@
             for i in range(16):
                 norm_copy(i).wait_recv()
         if t == 6:
-            for i in (3, 4, 5, 8):
+            for i in (2, 3, 4, 5, 8):
                 local[i].wait()
+            lora = jnp.dot(low2[...].astype(jnp.bfloat16), up_ref[...], preferred_element_type=jnp.float32)
+            acc[mine, :512] += ADAPTER_SCALE * lora
+            for half in range(2):
+                rows = slice(half * 128, half * 128 + 128)
+                factor = spread(adv_ref, half, row, jnp.float32) / spread(len_ref, half, row, jnp.float32)
+                live = (row % 32) < spread(len_ref, half, row, jnp.int32)
+                for h in heads:
+                    weighted = (og_ref[rows, h].astype(jnp.float32) * factor).astype(jnp.bfloat16)
+                    og_ref[rows, h] = jnp.where(live, weighted.astype(jnp.float32), 0.0).astype(jnp.bfloat16)
             for r in range(8):
                 flags[me_d, pl.ds(r, 1), :] = jnp.full((1, 128), assign_ref[r], jnp.int32)
             for copy in flag_copies:
@@ -306,27 +328,13 @@
 
     low = low2[...].astype(jnp.bfloat16)
     low_wide = jnp.concatenate([low, low], axis=1)
-    lora = jnp.dot(low, up_ref[...], preferred_element_type=jnp.float32)
-    row = lax.broadcasted_iota(jnp.int32, (128, 128), 0)
-    col = lax.broadcasted_iota(jnp.int32, (128, 128), 1)
-    same = (row // 32) == (col // 32)
-    causal = same & ((col % 32) <= (row % 32))
-    scale = 128 ** (-0.5)
-    heads = [slice(h * 128, h * 128 + 128) for h in range(4)]
-
-    def spread(ref, half, where, kind):
-        out = jnp.full((128, 128), ref[half * 4].astype(kind), kind)
-        for r in range(1, 4):
-            out = jnp.where(where // 32 == r, jnp.full((128, 128), ref[half * 4 + r].astype(kind), kind), out)
-        return out
-
     lives = [(row % 32) < spread(len_ref, half, row, jnp.int32) for half in range(2)]
     seen = [causal & ((col % 32) < spread(len_ref, half, col, jnp.int32)) for half in range(2)]
     for half in range(2):
         rows = slice(half * 128, half * 128 + 128)
         part_copy(half).wait_recv()
         projected = acc[rows, :] + part_acc[rows, :]
-        queries = (projected[:, :512] + ADAPTER_SCALE * lora[rows, :]).astype(jnp.bfloat16)
+        queries = projected[:, :512].astype(jnp.bfloat16)
         keys = projected[:, 512:640].astype(jnp.bfloat16)
         values = projected[:, 640:].astype(jnp.bfloat16)
         kbuf[rows, :] = keys
@@ -341,32 +349,10 @@
             out = jnp.where(lives[half], outs[i], 0.0).astype(jnp.bfloat16)
             attb[half * 4 : half * 4 + 4, :, h] = out.reshape(4, 32, 128)
 
-    def fill_slot(d, carry):
-        which = jnp.int32(0)
-        for r in range(1, 8):
-            which = jnp.where(assign_ref[r] == d, jnp.int32(r), which)
-        pay_s[d] = attb[which]
-        return carry
-
-    lax.fori_loop(0, 16, fill_slot, 0)
-    rec_s[me_d] = pay_s[me_d]
-    slot_copies = [
-        pltpu.make_async_remote_copy(
-            src_ref=pay_s.at[(me_d + ORDER[i]) % 16], dst_ref=rec_s.at[me_d], send_sem=ssem.at[i],
-            recv_sem=srecv.at[i], device_id=((me_d + ORDER[i]) % 16, me_f), device_id_type=MESH,
-        )
-        for i in range(15)
-    ]
-    for copy in slot_copies[:SPLIT]:
-        copy.start()
-
-    local[2].wait()
     for half in range(2):
         rows = slice(half * 128, half * 128 + 128)
-        factor = spread(adv_ref, half, row, jnp.float32) / spread(len_ref, half, row, jnp.float32)
         keys, values = kbuf[rows, :], vbuf[rows, :]
-        weighted = [(og_ref[rows, h].astype(jnp.float32) * factor).astype(jnp.bfloat16) for h in heads]
-        weighted = [jnp.where(lives[half], w.astype(jnp.float32), 0.0).astype(jnp.bfloat16) for w in weighted]
+        weighted = [og_ref[rows, h] for h in heads]
         dsoft = [lax.dot_general(w, values, NT, preferred_element_type=jnp.float32) for w in weighted]
         dsoft = [d.astype(jnp.bfloat16).astype(jnp.float32) for d in dsoft]
         soft = [pbuf[half * 4 + i] for i in range(4)]
@@ -386,6 +372,24 @@
     up_four = up_grad.reshape(16, 2, 16, 128)
     lane = lax.broadcasted_iota(jnp.int32, (16, 16, 128), 2)
     ordered[...] = jnp.where(lane < 64, up_four[:, 0], up_four[:, 1]).astype(jnp.bfloat16)
+    def fill_slot(d, carry):
+        which = jnp.int32(0)
+        for r in range(1, 8):
+            which = jnp.where(assign_ref[r] == d, jnp.int32(r), which)
+        pay_s[d] = attb[which]
+        return carry
+
+    lax.fori_loop(0, 16, fill_slot, 0)
+    rec_s[me_d] = pay_s[me_d]
+    slot_copies = [
+        pltpu.make_async_remote_copy(
+            src_ref=pay_s.at[(me_d + ORDER[i]) % 16], dst_ref=rec_s.at[me_d], send_sem=ssem.at[i],
+            recv_sem=srecv.at[i], device_id=((me_d + ORDER[i]) % 16, me_f), device_id_type=MESH,
+        )
+        for i in range(15)
+    ]
+    for copy in slot_copies[:SPLIT]:
+        copy.start()
     lg_copy.wait()
 
     def down_slice(i, carry):
@@ -403,7 +407,7 @@
         y_to = y + other * ((y_cross if q % 2 else y_pair) - y)
         return pltpu.make_async_remote_copy(
             src_ref=pay_a.at[there, span], dst_ref=rec_a.at[k - 1, span], send_sem=asem.at[q, k - 1],
-            recv_sem=arecv.at[q, k - 1], device_id=at(z, y_to, there % 4), device_id_type=MESH,
+            recv_sem=arecv.at[q], device_id=at(z, y_to, there % 4), device_id_type=MESH,
         )
 
     chunks = range(16 // CHUNK)
@@ -411,6 +415,32 @@
         lax.fori_loop(q * CHUNK, (q + 1) * CHUNK, down_slice, 0)
         for k in range(1, 8):
             a_copy(q, k).start()
+    def slice_at(i):
+        return (z + Z_ORDER[i // 2]) % 8 * 2 + i % 2
+
+    def b_copy(i):
+        slot = i - i % 2 + yh if i < 14 else 14
+        return pltpu.make_async_remote_copy(
+            src_ref=pay_b.at[i if i < 14 else 15 - yh], dst_ref=rec_b.at[slot], send_sem=bsem.at[i],
+            recv_sem=brecv.at[0], device_id=(slice_at(i) if i < 14 else 2 * z + 1 - yh, me_f), device_id_type=MESH,
+        )
+
+    for q in chunks:
+        span = pl.ds(q * CHUNK, CHUNK)
+        arrived = rec_a.at[:, span]
+        pltpu.make_async_copy(arrived, arrived, arecv.at[q]).wait()
+        total = pay_a[chip, span].astype(jnp.float32)
+        for k in range(7):
+            total += rec_a[k, span].astype(jnp.float32)
+        pay_b[span, 0] = total.astype(jnp.bfloat16)
+        for i in range(q * CHUNK, (q + 1) * CHUNK):
+            pay_b[i, 1] = ordered[slice_at(i)]
+            if i < 14:
+                b_copy(i).start()
+    b_copy(14).start()
+
+    for copy in slot_copies[SPLIT:]:
+        copy.start()
     for e in range(N_ENTRIES):
         piece_send(e).wait_send()
     for i in range(16):
@@ -422,32 +452,9 @@
             pass_on(i, v).wait_send()
     for copy in flag_copies:
         copy.wait()
-    def slice_at(i):
-        return (z + Z_ORDER[i // 2]) % 8 * 2 + i % 2
-
-    def b_copy(i):
-        slot = i - i % 2 + yh if i < 14 else 14
-        return pltpu.make_async_remote_copy(
-            src_ref=pay_b.at[i if i < 14 else 15 - yh], dst_ref=rec_b.at[slot], send_sem=bsem.at[i],
-            recv_sem=brecv.at[0], device_id=(slice_at(i) if i < 14 else 2 * z + 1 - yh, me_f), device_id_type=MESH,
-        )
-
     for q in chunks:
-        span = pl.ds(q * CHUNK, CHUNK)
         for k in range(1, 8):
-            a_copy(q, k).wait()
-        total = pay_a[chip, span].astype(jnp.float32)
-        for k in range(7):
-            total += rec_a[k, span].astype(jnp.float32)
-        pay_b[span, 0] = total.astype(jnp.bfloat16)
-        for i in range(q * CHUNK, (q + 1) * CHUNK):
-            pay_b[i, 1] = ordered[slice_at(i)]
-            if i < 14:
-                b_copy(i).start()
-    b_copy(14).start()
-
-    for copy in slot_copies[SPLIT:]:
-        copy.start()
+            a_copy(q, k).wait_send()
     pltpu.make_async_copy(rec_b, rec_b, brecv.at[0]).wait()
     total = pay_b[14 + yh].astype(jnp.float32)
     for k in range(15):
@@ -549,7 +556,7 @@
             pltpu.VMEM((2, 16, 128), bf16),
             pltpu.SemaphoreType.REGULAR((5,)),
             dma((32,)), dma((11,)), dma((N_ENTRIES,)), dma((N_ENTRIES,)), dma((4 * len(LATE),)), dma((4 * len(LATE),)),
-            dma((2, 19)), dma((15,)), dma((15,)), dma((15,)), dma((15,)), dma((16 // CHUNK, 7)), dma((16 // CHUNK, 7)),
+            dma((2, 19)), dma((15,)), dma((15,)), dma((15,)), dma((15,)), dma((16 // CHUNK, 7)), dma((16 // CHUNK,)),
             dma((15,)), dma((1,)), dma((1,)), dma((1,)),
         ],
         compiler_params=pltpu.CompilerParams(

time: 64.8 us -> 64.2 us (level)
  no operation moved by 1% of the time
where the time goes in v7:
time: 64.2 us; the launch traced here: 64.1 us
  Pallas kernels  63.4 us (99%)
    pallas_call x1, Pallas kernels, on_device(): pl.pallas_call(kernel, out_shape=(jax.ShapeDtypeStruct((8, 32, 512), bf16...  61.7 us
    pallas_call x1, Pallas kernels, on_device(): pl.pallas_call(assemble, out_shape=(jax.ShapeDtypeStruct((8, 32, 512), bf...  1.75 us

profile of v7, /device:TPU:1, one launch (start us, length us, event | category | flops | bytes accessed | tf_op | source)
XLA Modules:
  0.0 64.1 jit_solution(15434588735812312900)
XLA Ops:
  0.6 61.7 %block.1 = (bf16[8,32,512]{2,1,0:T(8,128)(2,1)}, bf16[16,2,16,128]{3,2,1,0:T(8,128)(2,1)}) custom-call(s32[8]{0:T(128)} %len_hbm.1, s32[8]{0:T(128)} %assign_hbm.1, f32[8]{0:T(128)} %adv_hbm.1, bf16[256,8192]{1,0:T(8,128)(2,1)} %bitcast.6, f32[1,8192]{1,0:T(1,128)} %bitcast.9, bf16[512,768]{1,0:T(8,128)(2,1)} %w_ref.1, bf16[768]{0:T(1024)(128)(2,1)} %bias_hbm.1, ...), custom_call_target="tpu_custom_call" | custom-call | tf_op jit(solution)/shard_map/block/pallas_call | solution.py:520
  62.3 1.8 %assemble.1 = (bf16[8,32,512]{2,1,0:T(8,128)(2,1)}, f32[64,512]{1,0:T(8,128)}, f32[32,64]{1,0:T(8,128)}) custom-call(bf16[8,32,512]{2,1,0:T(8,128)(2,1)} %get-tuple-element.8.att_ref, bf16[16,2,16,128]{3,2,1,0:T(8,128)(2,1)} %get-tuple-element.9.sums_ref), custom_call_target="tpu_custom_call" | custom-call | tf_op jit(solution)/shard_map/assemble/pallas_call | solution.py:578
